TPU v7x, 32 devices: a whole 2x2x4 slice. The times are simulated.
32 devices in a mesh: seq: 8 (over z, x), tp: 4 (over y, core).
Axes of the slice: x: 2, y: 2, z: 4, core: 2. Of those that a mesh axis runs over, the one named last changes fastest.
Arguments:
- hidden_in: bfloat16 [2048, 1536], P('seq', 'tp'), may hold values from -6 to 6
- w_in_gate: float32 [1536, 3072], P('seq', 'tp'), may hold values from -0.15625 to 0.15625
- w_in_value: float32 [1536, 3072], P('seq', 'tp'), may hold values from -0.15625 to 0.15625
- w_in_shared: float32 [1536, 256], P('seq'), may hold values from -0.15625 to 0.15625
- w_in_step: float32 [1536, 48], P('seq', 'tp'), may hold values from -0.15625 to 0.15625
- conv_value: float32 [4, 3072], P(None, 'tp'), may hold values from -3 to 3
- conv_shared: float32 [4, 256], replicated, may hold values from -3 to 3
- dt_bias: float32 [48], P('tp'), may hold values from -4 to -2
- a_log: float32 [48], P('tp'), may hold values from -8 to 0
- skip_gain: float32 [48], P('tp'), may hold values from 0.6 to 4.8
- norm_gain: float32 [3072], P('tp'), may hold values from 0.1 to 1.9
- w_out: float32 [3072, 1536], P('tp', 'seq'), may hold values from -0.109375 to 0.109375
- prompt_lengths: int32 [8], replicated, may hold values from 1 to 1024, 2048 in all
- row_blocks: int32 [8], replicated, may hold values from 0 to 7, each once
Outputs:
- mixed_out: bfloat16 [2048, 1536], P('seq', 'tp')
Inputs may be any that keep to these rules, and one draw needn't show every extreme that they name: `prompt_lengths`: 8 lengths that sum to 2048, the longest exactly 1024. `row_blocks`: a permutation of the row blocks.
All inputs are finite; a program needn't handle non-finite values.
Results may differ from a plain program's by a relative error of at most 0.02.
Values may be sent and summed in bfloat16 or wider, within the bound.
A program may use at most 128 MiB of HBM per device.

v0:
```python
import jax
import jax.numpy as jnp
from jax import lax
from jax.sharding import PartitionSpec as P

EPSILON = 1e-05
HIGHEST_PREC = lax.Precision.HIGHEST


def passed_along(block, axis, distance):
    devices = range(lax.axis_size(axis))
    route = [(i - distance, i) for i in devices if i - distance in devices]
    return lax.ppermute(block, axis, route)


def prefix_2(x, axis, combine, identity):
    count, here = (lax.axis_size(axis), lax.axis_index(axis))
    everything = jax.tree.map(
        lambda part, kind: lax.all_gather(part.astype(kind), axis), x, (jnp.bfloat16, jnp.bfloat16)
    )
    start = jax.tree.map(
        lambda part, zero: jnp.broadcast_to(jnp.asarray(zero, part.dtype), part.shape), x, identity
    )

    def turn(k, before):
        reached = k < here
        new = combine(
            before, jax.tree.map(lambda part, own: part[k].astype(own.dtype), everything, x)
        )
        return jax.tree.map(lambda a, b: jnp.where(reached, a, b), new, before)

    return lax.fori_loop(0, count, turn, start)


def segment_of(positions, doc_ends):
    return jnp.sum((positions[:, None] >= doc_ends[None, :]).astype(jnp.int32), axis=1)


def span_parts(values, b_half, c_half, steps_dt, decay_rates, segments, prev_seg):
    length = values.shape[0]
    b_rows = b_half.astype(jnp.float32)
    cumulative = jnp.cumsum(-steps_dt * decay_rates[None, :], axis=0)
    places = jnp.arange(length)
    causal = (places[:, None] >= places[None, :]) & (segments[:, None] == segments[None, :])
    gaps_log = jnp.where(causal[:, :, None], cumulative[:, None, :] - cumulative[None, :, :], 0.0)
    decays_in = jnp.where(causal[:, :, None], jnp.exp(gaps_log), 0.0)
    scores = jnp.dot(c_half, b_half.T, preferred_element_type=jnp.float32)
    weights = scores[:, :, None] * decays_in * steps_dt[None, :, :]
    intra_part = jnp.einsum("ijh,jhp->ihp", weights, values, precision=HIGHEST_PREC)
    carry_in = jnp.where((segments == prev_seg)[:, None], jnp.exp(cumulative), 0.0)
    tail_weight = (
        jnp.where(
            (segments == segments[-1])[:, None], jnp.exp(cumulative[-1][None, :] - cumulative), 0.0
        )
        * steps_dt
    )
    fresh_state = jnp.einsum("jh,jhp,jn->hpn", tail_weight, values, b_rows, precision=HIGHEST_PREC)
    keep_factor = jnp.where(segments[-1] == prev_seg, jnp.exp(cumulative[-1]), 0.0)
    return (intra_part, carry_in, fresh_state, keep_factor)


def combine(earlier, later):
    return (earlier[0] * later[0], later[0][:, None, None] * earlier[1] + later[1])


def on_device(
    hidden_in,
    w_in_gate,
    w_in_value,
    w_in_shared,
    w_in_step,
    conv_value,
    conv_shared,
    dt_bias,
    a_log,
    skip_gain,
    norm_gain,
    w_out,
    prompt_lengths,
    row_blocks,
):
    seq_count = lax.axis_size("seq")
    tokens_here = hidden_in.shape[0]
    edge_count = conv_value.shape[0] - 1
    gathered = lax.all_gather(hidden_in, "tp", axis=1, tiled=True)
    row_count = gathered.shape[0]
    model_width = gathered.shape[1]
    permuted = jnp.take(
        gathered.reshape(row_count, seq_count, model_width // seq_count), row_blocks, axis=1
    ).reshape(row_count, model_width)
    stored = (
        w_in_gate.astype(jnp.bfloat16),
        w_in_value.astype(jnp.bfloat16),
        w_in_shared.astype(jnp.bfloat16),
        w_in_step.astype(jnp.bfloat16),
    )
    pieces = (
        lax.all_gather(stored[0], "seq", axis=0, tiled=True),
        lax.all_gather(stored[1], "seq", axis=0, tiled=True),
        lax.all_gather(stored[2], "seq", axis=0, tiled=True),
        lax.all_gather(stored[3], "seq", axis=0, tiled=True),
    )
    projected = tuple(
        (
            jnp.dot(permuted, weight_piece, preferred_element_type=jnp.float32)
            for weight_piece in pieces
        )
    )
    gate_all, value_all, shared_all, raw_all = [result.astype(jnp.bfloat16) for result in projected]
    mixed_in = jnp.concatenate([value_all, shared_all], axis=1)
    edge_mix = passed_along(mixed_in[tokens_here - edge_count :], "seq", 1)
    doc_ends = jnp.cumsum(prompt_lengths)
    first_pos = lax.axis_index("seq") * tokens_here
    positions = first_pos + jnp.arange(tokens_here, dtype=jnp.int32)
    edge_positions = first_pos - edge_count + jnp.arange(edge_count, dtype=jnp.int32)
    segments = segment_of(positions, doc_ends)
    ext_segments = jnp.concatenate([segment_of(edge_positions, doc_ends), segments])
    ext_rows = jnp.concatenate([edge_mix, mixed_in], axis=0)
    kernel = jnp.concatenate([conv_value, conv_shared], axis=1)
    conv_sum = jnp.zeros(mixed_in.shape, jnp.float32)
    for tap_index in range(edge_count + 1):
        same_doc = (ext_segments[tap_index : tap_index + tokens_here] == segments)[:, None]
        conv_sum = conv_sum + jnp.where(
            same_doc,
            kernel[tap_index][None, :]
            * ext_rows[tap_index : tap_index + tokens_here].astype(jnp.float32),
            0.0,
        )
    convolved = jax.nn.silu(conv_sum).astype(jnp.bfloat16)
    local_inner = conv_value.shape[1]
    local_heads = dt_bias.shape[0]
    head_dim = local_inner // local_heads
    state_size = conv_shared.shape[1] // 2
    values = (
        convolved[:, :local_inner].astype(jnp.float32).reshape(tokens_here, local_heads, head_dim)
    )
    b_half = convolved[:, local_inner : local_inner + state_size]
    c_half = convolved[:, local_inner + state_size :]
    c_rows = c_half.astype(jnp.float32)
    steps_dt = jax.nn.softplus(raw_all.astype(jnp.float32) + dt_bias[None, :])
    decay_rates = jnp.exp(a_log)
    prev_first = segment_of(jnp.reshape(first_pos - 1, (1,)), doc_ends)[0]
    device_keep = jnp.ones((local_heads,), jnp.float32)
    device_state = jnp.zeros((local_heads, head_dim, state_size), jnp.float32)
    parts = span_parts(values, b_half, c_half, steps_dt, decay_rates, segments, prev_first)
    device_keep = parts[3] * device_keep
    device_state = parts[3][:, None, None] * device_state + parts[2]
    identity = (jnp.ones_like(device_keep), jnp.zeros_like(device_state))
    prefix = prefix_2((device_keep, device_state), "seq", combine, identity)
    carried = prefix[1]
    intra_part, carry_in, fresh_state, keep_factor = parts
    inter_part = (
        jnp.einsum("in,hpn->ihp", c_rows, carried, precision=HIGHEST_PREC) * carry_in[:, :, None]
    )
    outputs = intra_part + inter_part
    mixed_heads = outputs + skip_gain[None, :, None] * values
    gated = mixed_heads.reshape(tokens_here, local_inner) * jax.nn.silu(
        gate_all.astype(jnp.float32)
    )
    squares = jnp.sum(gated * gated, axis=1)
    square_total = lax.psum(squares, "tp")
    mean_square = square_total / (local_inner * lax.axis_size("tp"))
    normed = (gated * lax.rsqrt(mean_square + EPSILON)[:, None] * norm_gain[None, :]).astype(
        jnp.bfloat16
    )
    out_weight = w_out.astype(jnp.bfloat16)
    partial_terms = jnp.dot(
        normed,
        lax.all_gather(out_weight, "seq", axis=1, tiled=True),
        preferred_element_type=jnp.float32,
    )
    return lax.psum_scatter(
        partial_terms.astype(jnp.bfloat16), "tp", scatter_dimension=1, tiled=True
    )


def solution(mesh):
    return jax.shard_map(
        on_device,
        mesh=mesh,
        in_specs=(
            P("seq", "tp"),
            P("seq", "tp"),
            P("seq", "tp"),
            P("seq", None),
            P("seq", "tp"),
            P(None, "tp"),
            P(),
            P("tp"),
            P("tp"),
            P("tp"),
            P("tp"),
            P("tp", "seq"),
            P(),
            P(),
        ),
        out_specs=P("seq", "tp"),
        check_vma=False,
    )
```

profile of v0, /device:TPU:29, one launch (start us, length us, event | category | flops | bytes accessed | tf_op | source)
XLA Modules:
  0.0 286.2 jit_solution(16293368399873254822)
XLA Ops:
  6.5 1.8 convert_element_type.112
  10.6 1.1 copy.35
  13.5 21.7 %all-gather.1 = bf16[8,192,12]{1,2,0:T(8,128)(2,1)S(1)} all-gather(bf16[1,192,12]{1,2,0:T(8,128)(2,1)S(1)} %convert_bitcast_fusion), channel_id=1, replica_groups=mesh['seq'=8,'tp'=4] {'seq'}, dimensions={0}, use_global_device_ids=true | all-gather | bytes 41472 | tf_op jit(solution)/shard_map/all_gather | solution.py:101
  36.7 14.3 %all_gather.28 = bf16[256,1536]{0,1:T(8,128)(2,1)S(1)} all-gather(bf16[256,384]{0,1:T(8,128)(2,1)S(1)} %copy.35), channel_id=1, replica_groups=mesh['seq'=8,'tp'=4] {'tp'}, dimensions={1}, use_global_device_ids=true | all-gather | bytes 983040 | tf_op jit(solution)/shard_map/all_gather | solution.py:85
  55.4 1.3 broadcast_compare_fusion
  56.8 26.2 %all_gather.30 = bf16[1536,256]{1,0:T(8,128)(2,1)S(1)} all-gather(bf16[192,256]{1,0:T(8,128)(2,1)S(1)} %convert_element_type.114), channel_id=1, replica_groups=mesh['seq'=8,'tp'=4] {'seq'}, dimensions={0}, use_global_device_ids=true | all-gather | bytes 884736 | tf_op jit(solution)/shard_map/all_gather | solution.py:100
  83.4 2.5 convolution_convert_fusion.2
  85.9 5.5 %collective-permute-start = (bf16[3,1024]{1,0:T(4,128)(2,1)S(1)}, bf16[3,1024]{1,0:T(4,128)(2,1)S(1)}, u32[]{:S(2)}, u32[]{:S(2)}) collective-permute-start(bf16[3,1024]{1,0:T(4,128)(2,1)S(1)} %fusion.40), channel_id=1, source_target_pairs={{0,4},{4,8},{8,12},{12,16},{16,20},{20,24},{24,28},{1,5},{5,9},{9,... | collective-permute-start | bytes 18440 | tf_op jit(solution)/shard_map/ppermute | solution.py:13
  93.4 1.2 fusion.20
  96.7 12.6 %all-gather.2 = bf16[8,1,12]{2,1,0:T(2,128)(2,1)S(1)} all-gather(bf16[1,1,12]{2,1,0:T(2,128)(2,1)S(1)} %bitcast.95), channel_id=1, replica_groups=mesh['seq'=8,'tp'=4] {'seq'}, dimensions={0}, use_global_device_ids=true | all-gather | bytes 216 | tf_op jit(solution)/shard_map/all_gather | solution.py:19
  109.5 3.6 %fusion.14 = f32[256,12,64]{0,2,1:T(8,128)} fusion(bf16[256,12,64]{0,2,1:T(8,128)(2,1)S(1)} %bitcast.79, f32[256,12]{0,1:T(8,128)S(1)} %get-tuple-element.130, f32[256,12]{0,1:T(8,128)S(1)} %bitcast.88, f32[256,256]{1,0:T(8,128)S(1)} %fusion.30, pred[256,256]{1,0:T(8,128)(4,1)S(1)} %fusion.26), kind=kOutput, calls=%fused_computation.18 | convolution fusion | flops 607911936 | bytes 1531904 | tf_op jit(solution)/shard_map/ijh,jhp->ihp/dot_general | solution.py:49
  113.0 33.3 %all-gather.14.cloned.1.call-done = bf16[96,64,128]{2,1,0:T(8,128)(2,1)} async-done(((bf16[12,64,128]{2,1,0:T(8,128)(2,1)}), bf16[96,64,128]{2,1,0:T(8,128)(2,1)}) %all-gather.14.cloned.1.call-update) | async-done | bytes 1572880 | tf_op jit(solution)/shard_map/all_gather | solution.py:19
  146.3 8.7 %while.14 = (s32[]{:T(128)}, f32[12,64,128]{2,1,0:T(8,128)S(1)}, s32[]{:T(128)}, bf16[8,12]{1,0:T(8,128)(2,1)S(1)}, bf16[8,12,64,128]{3,2,1,0:T(8,128)(2,1)}, /*index=5*/s32[]{:T(128)}, s32[]{:T(128)}) while((s32[]{:T(128)}, f32[12,64,128]{2,1,0:T(8,128)S(1)}, s32[]{:T(128)}, bf16[8,12]{1,0:T(8,128)(2,1)S(1)}, ...), condition=%wide.region_7.8_spmd.clone, body=%wide.region_6.7_spmd.clone.sunk | while | flops 491536 | bytes 983265 | solution.py:32
  146.3 1.1 fusion.58
  147.4 1.1 fusion.58
  155.0 1.6 fusion.18
  156.9 42.1 %all-gather.10.cloned.1.call-done = bf16[1536,768]{1,0:T(8,128)(2,1)} async-done(((bf16[192,768]{1,0:T(8,128)(2,1)}), bf16[1536,768]{1,0:T(8,128)(2,1)}) %all-gather.10.cloned.1.call-update) | async-done | bytes 2359312 | tf_op jit(solution)/shard_map/all_gather | solution.py:98
  199.0 2.7 multiply_reduce_fusion
  201.7 5.8 %psum.7 = f32[256]{0:T(256)S(1)} all-reduce(f32[256]{0:T(256)S(1)} %get-tuple-element.145), channel_id=1, replica_groups=mesh['seq'=8,'tp'=4] {'tp'}, use_global_device_ids=true, to_apply=%region_9.10 | all-reduce | flops 256 | bytes 2048 | tf_op jit(solution)/shard_map/psum | solution.py:161
  207.5 44.2 %all-gather.12.cloned.1.call-done = bf16[768,1536]{0,1:T(8,128)(2,1)} async-done(((bf16[768,192]{0,1:T(8,128)(2,1)}), bf16[768,1536]{0,1:T(8,128)(2,1)}) %all-gather.12.cloned.1.call-update) | async-done | bytes 2359312 | tf_op jit(solution)/shard_map/all_gather | solution.py:169
  251.7 2.5 convolution_convert_fusion
  254.2 1.2 copy.43
  255.4 22.6 %reduce-scatter.4.cloned.1.call-done = bf16[384,256]{1,0:T(8,128)(2,1)} async-done(((bf16[1536,256]{1,0:T(8,128)(2,1)}), bf16[384,256]{1,0:T(8,128)(2,1)}) %reduce-scatter.4.cloned.1.call-update) | async-done | bytes 196624
  278.0 1.7 copy.44
  (92 shorter events, 19.9 us)
Async XLA Ops:
  6.5 76.9 %all-gather.8.cloned.1.call-start = ((), (), s32[]{:S(2)}) async-start(), calls=%async_computation.1 | async-start | bytes 2654208 | tf_op jit(solution)/shard_map/all_gather | solution.py:99
  8.4 137.9 %all-gather.14.cloned.1.call-start = ((), (), s32[]{:S(2)}) async-start(), calls=%async_computation.4 | async-start | bytes 1769472 | tf_op jit(solution)/shard_map/all_gather | solution.py:19
  35.2 16.7 %copy-start.5 = (f32[12]{0:T(128)S(1)}, f32[12]{0:T(128)}, u32[]{:S(2)}) copy-start(f32[12]{0:T(128)} %param.23) | copy-start | bytes 148
  51.0 4.2 %copy-start.2 = (f32[4,768]{1,0:T(4,128)S(1)}, f32[4,768]{1,0:T(4,128)}, u32[]{:S(2)}) copy-start(f32[4,768]{1,0:T(4,128)} %param.21) | copy-start | bytes 36868
  51.0 4.2 %copy-start.4 = (f32[4,256]{1,0:T(4,128)S(1)}, f32[4,256]{1,0:T(4,128)}, u32[]{:S(2)}) copy-start(f32[4,256]{1,0:T(4,128)} %param.22) | copy-start | bytes 12292
  85.9 6.3 %collective-permute-start = (bf16[3,1024]{1,0:T(4,128)(2,1)S(1)}, bf16[3,1024]{1,0:T(4,128)(2,1)S(1)}, u32[]{:S(2)}, u32[]{:S(2)}) collective-permute-start(bf16[3,1024]{1,0:T(4,128)(2,1)S(1)} %fusion.40), channel_id=1, source_target_pairs={{0,4},{4,8},{8,12},{12,16},{16,20},{20,24},{24,28},{1,5},{5,9},{9,... | collective-permute-start | bytes 18440 | tf_op jit(solution)/shard_map/ppermute | solution.py:13
  92.4 2.3 copy-start
  93.2 2.3 copy-start.1
  94.7 104.4 %all-gather.10.cloned.1.call-start = ((), (), s32[]{:S(2)}) async-start(), calls=%async_computation.2 | async-start | bytes 2654208 | tf_op jit(solution)/shard_map/all_gather | solution.py:98
  95.5 156.2 %all-gather.12.cloned.1.call-start = ((), (), s32[]{:S(2)}) async-start(), calls=%async_computation.3 | async-start | bytes 2654208 | tf_op jit(solution)/shard_map/all_gather | solution.py:169
  96.3 181.6 %reduce-scatter.4.cloned.1.call-start = ((), (), s32[]{:S(2)}) async-start(), calls=%async_computation.5 | async-start | bytes 983040
  146.3 8.7 %copy-start.6 = (f32[12]{0:T(128)S(1)}, f32[12]{0:T(128)}, u32[]{:S(2)}) copy-start(f32[12]{0:T(128)} %param.25) | copy-start | bytes 148
  156.9 94.8 %copy-start.3 = (f32[768]{0:T(1024)S(1)}, f32[768]{0:T(1024)}, u32[]{:S(2)}) copy-start(f32[768]{0:T(1024)} %param.26) | copy-start | bytes 9220
Sparse Core Ops, SparseCore 0:
  9.5 51.5 all-gather.7
  94.8 51.4 all-gather.13
  148.5 50.4 all-gather.9
  201.1 50.5 all-gather.11
  255.5 22.3 reduce-scatter.3
where the time goes:
time: 290 us; the launch traced here: 286 us
  waiting for transfers between devices  143 us (49%)
  blocking collectives  80.6 us (28%)
  other arithmetic  20.2 us (7%)
  matrix products  14.9 us (5%)
  between operations  14.7 us (5%)
  local copies, waits for them, and re-layouts  6.99 us (2%)
  starting transfers between devices  5.72 us (2%)
    all_gather x1, waiting for transfers between devices, on_device(): lax.all_gather(out_weight, 'seq', axis=1, tiled=True)  44.2 us
    all_gather x1, waiting for transfers between devices, on_device(): lax.all_gather(stored[0], 'seq', axis=0, tiled=True)  42.1 us
    all_gather x1, waiting for transfers between devices, prefix_2(): lax.all_gather(part.astype(kind), axis)  33.3 us
    all_gather x1, blocking collectives, on_device(): lax.all_gather(stored[2], 'seq', axis=0, tiled=True)  26.2 us
    unnamed x6, waiting for transfers between devices  22.6 us
    all_gather x1, blocking collectives, on_device(): lax.all_gather(stored[3], 'seq', axis=0, tiled=True)  21.7 us
    all_gather x1, blocking collectives, on_device(): gathered = lax.all_gather(hidden_in, 'tp', axis=1, tiled=True)  14.3 us
    all_gather x1, blocking collectives, prefix_2(): lax.all_gather(part.astype(kind), axis)  12.6 us
  transfers between devices with their start and end apart: 6, of which 5 were waited for; matrix products, arithmetic and copies ran while one was open for 10% of the time, Pallas kernels for 0%

commit v1 on v0

--- a/solution.py
+++ b/solution.py
@@ -1,7 +1,14 @@
+import functools
+
 import jax
 import jax.numpy as jnp
 from jax import lax
+from jax.experimental import pallas as pl
+from jax.experimental.pallas import tpu as pltpu
 from jax.sharding import PartitionSpec as P
+
+MESH = pl.DeviceIdType.MESH
+ROWS_AT_ONCE = 48
 
 EPSILON = 1e-05
 HIGHEST_PREC = lax.Precision.HIGHEST
@@ -63,7 +70,7 @@
     return (earlier[0] * later[0], later[0][:, None, None] * earlier[1] + later[1])
 
 
-def on_device(
+def on_device_plain(
     hidden_in,
     w_in_gate,
     w_in_value,
@@ -174,9 +181,509 @@
     )
 
 
+def place():
+    seq, tp = lax.axis_index("seq"), lax.axis_index("tp")
+    return seq, tp, seq // 2, seq % 2, tp // 2, tp % 2
+
+
+def remote(src, dst, send, recv, seq, tp):
+    return pltpu.make_async_remote_copy(
+        src_ref=src, dst_ref=dst, send_sem=send, recv_sem=recv,
+        device_id=(seq, tp), device_id_type=MESH,
+    )
+
+
+def greet_plane(planes):
+    seq, tp, z, x, y, c = place()
+    barrier = pltpu.get_barrier_semaphore()
+    for other in range(1, 8):
+        dx, dt = other // 4, other % 4
+        pl.semaphore_signal(
+            barrier, inc=1, device_id=(2 * z + (x + dx) % 2, (tp + dt) % 4), device_id_type=MESH
+        )
+
+    if planes > 1:
+        @pl.when(z > 0)
+        def _():
+            pl.semaphore_signal(barrier, inc=1, device_id=(seq - 2, tp), device_id_type=MESH)
+
+        @pl.when(z < planes - 1)
+        def _():
+            pl.semaphore_signal(barrier, inc=1, device_id=(seq + 2, tp), device_id_type=MESH)
+
+    extra = (0 if planes == 1 else 1) + jnp.where((z > 0) & (z < planes - 1), 1, 0)
+    pl.semaphore_wait(barrier, 7 + extra)
+
+
+def gather_kernel(
+    planes, h_ref, w_ref, p_ref, hid_ref, all_ref, par_ref,
+    got, swapped, up, down, across, h_send, h_got, p_sems,
+):
+    seq, tp, z, x, y, c = place()
+    chunks = w_ref.shape[0] // ROWS_AT_ONCE
+    mine = 2 * z + c
+    greet_plane(planes)
+
+    def rows(k):
+        return pl.ds(pl.multiple_of(k * ROWS_AT_ONCE, ROWS_AT_ONCE), ROWS_AT_ONCE)
+
+    def local_part(k):
+        return pltpu.make_async_copy(w_ref.at[rows(k)], all_ref.at[mine, rows(k)], got.at[mine, k])
+
+    def swap_part(k):
+        slot = 2 * z + 1 - c
+        return remote(
+            w_ref.at[rows(k)], all_ref.at[slot, rows(k)], swapped.at[k], got.at[slot, k],
+            seq + 1 - 2 * x, tp + 1 - 2 * c,
+        )
+
+    def landed(slot, k):
+        here = all_ref.at[slot, rows(k)]
+        return remote(here, here, swapped.at[k], got.at[slot, k], seq, tp + 1 - 2 * c)
+
+    def sent(slot, k, sems, to_seq, to_tp):
+        here = all_ref.at[slot, rows(k)]
+        return remote(here, here, sems.at[slot // 2, k], got.at[slot, k], to_seq, to_tp)
+
+    par_local = pltpu.make_async_copy(p_ref, par_ref, p_sems.at[0])
+    par_swap = remote(p_ref, par_ref, p_sems.at[1], p_sems.at[0], seq + 1 - 2 * x, tp + 1 - 2 * c)
+
+    @pl.when(x == c)
+    def _():
+        @pl.loop(0, chunks)
+        def _(k):
+            local_part(k).start()
+        par_local.start()
+
+    @pl.when(x != c)
+    def _():
+        @pl.loop(0, chunks)
+        def _(k):
+            swap_part(k).start()
+        par_swap.start()
+
+    def features(to):
+        return remote(
+            h_ref, hid_ref.at[tp], h_send.at[to], h_got.at[tp], 2 * z + to // 2, 2 * (to % 2) + x
+        )
+
+    own_features = pltpu.make_async_copy(h_ref, hid_ref.at[tp], h_got.at[tp])
+    for to in range(4):
+        itself = (x == c) & (x == to // 2) & (y == to % 2)
+
+        @pl.when(itself)
+        def _():
+            own_features.start()
+
+        @pl.when(jnp.logical_not(itself))
+        def _():
+            features(to).start()
+
+    def hand_on(slot, k, going_up, going_down):
+        if going_up:
+            @pl.when(z < planes - 1)
+            def _():
+                sent(slot, k, up, seq + 2, tp).start()
+        if going_down:
+            @pl.when(z > 0)
+            def _():
+                sent(slot, k, down, seq - 2, tp).start()
+        sent(slot, k, across, seq, tp + 1 - 2 * c).start()
+
+    @pl.loop(0, chunks)
+    def _(k):
+        @pl.when(x == c)
+        def _():
+            local_part(k).wait()
+
+        @pl.when(x != c)
+        def _():
+            landed(mine, k).wait_recv()
+
+        hand_on(mine, k, True, True)
+
+    for far in range(1, planes):
+        @pl.loop(0, chunks)
+        def _(k):
+            @pl.when(z >= far)
+            def _():
+                landed(mine - 2 * far, k).wait_recv()
+                hand_on(mine - 2 * far, k, True, False)
+
+            @pl.when(z < planes - far)
+            def _():
+                landed(mine + 2 * far, k).wait_recv()
+                hand_on(mine + 2 * far, k, False, True)
+
+    @pl.loop(0, chunks)
+    def _(k):
+        for at in range(planes):
+            slot = 2 * at + c
+            landed(2 * at + 1 - c, k).wait_recv()
+            sent(slot, k, across, seq, tp + 1 - 2 * c).wait_send()
+
+            @pl.when((z < planes - 1) & (z >= at))
+            def _():
+                sent(slot, k, up, seq + 2, tp).wait_send()
+
+            @pl.when((z > 0) & (z <= at))
+            def _():
+                sent(slot, k, down, seq - 2, tp).wait_send()
+
+        @pl.when(x != c)
+        def _():
+            swap_part(k).wait_send()
+
+    for to in range(4):
+        itself = (x == c) & (x == to // 2) & (y == to % 2)
+
+        @pl.when(jnp.logical_not(itself))
+        def _():
+            features(to).wait_send()
+
+    for quarter in range(4):
+        remote(
+            h_ref, hid_ref.at[quarter], h_send.at[0], h_got.at[quarter], seq, tp + 1 - 2 * c
+        ).wait_recv()
+
+    @pl.when(x == c)
+    def _():
+        par_local.wait()
+
+    @pl.when(x != c)
+    def _():
+        par_swap.wait()
+
+
+def gather_all(hidden, packed, params, planes):
+    any_spec = pl.BlockSpec(memory_space=pl.ANY)
+    blocks, chunks = 2 * planes, packed.shape[0] // ROWS_AT_ONCE
+    dma = pltpu.SemaphoreType.DMA
+    return pl.pallas_call(
+        functools.partial(gather_kernel, planes),
+        out_shape=(
+            jax.ShapeDtypeStruct((4,) + hidden.shape, hidden.dtype),
+            jax.ShapeDtypeStruct((blocks,) + packed.shape, packed.dtype),
+            jax.ShapeDtypeStruct(params.shape, params.dtype),
+        ),
+        in_specs=[any_spec] * 3,
+        out_specs=[any_spec] * 3,
+        scratch_shapes=[
+            dma((blocks, chunks)), dma((chunks,)), dma((planes, chunks)), dma((planes, chunks)),
+            dma((planes, chunks)), dma((4,)), dma((4,)), dma((2,)),
+        ],
+        compiler_params=pltpu.CompilerParams(collective_id=0, has_side_effects=True),
+        name="gather_weights",
+    )(hidden, packed, params)
+
+
+def chain_kernel(planes, fresh_ref, keep_ref, state_ref, arrived, leaving, send, recv):
+    seq, tp, z, x, y, c = place()
+    first, last = (z == 0) & (c == 0), (z == planes - 1) & (c == 1)
+    before = (seq - 2 * (1 - c), tp + 1 - 2 * c)
+    after = (seq + 2 * c, tp + 1 - 2 * c)
+    barrier = pltpu.get_barrier_semaphore()
+
+    @pl.when(jnp.logical_not(first))
+    def _():
+        pl.semaphore_signal(barrier, inc=1, device_id=before, device_id_type=MESH)
+
+    @pl.when(jnp.logical_not(last))
+    def _():
+        pl.semaphore_signal(barrier, inc=1, device_id=after, device_id_type=MESH)
+
+    pl.semaphore_wait(barrier, jnp.where(first | last, 1, 2))
+    half = fresh_ref.shape[0] // 2
+    for part in range(2):
+        heads = pl.ds(part * half, half)
+
+        def onward():
+            return remote(
+                leaving.at[heads], arrived.at[heads], send.at[part], recv.at[part], *after
+            )
+
+        @pl.when(first)
+        def _():
+            state_ref[heads] = jnp.zeros((half,) + state_ref.shape[1:], jnp.float32)
+
+        @pl.when(jnp.logical_not(first))
+        def _():
+            remote(
+                leaving.at[heads], arrived.at[heads], send.at[part], recv.at[part], *before
+            ).wait_recv()
+            state_ref[heads] = arrived[heads].astype(jnp.float32)
+
+        @pl.when(jnp.logical_not(last))
+        def _():
+            leaving[heads] = (keep_ref[heads] * state_ref[heads] + fresh_ref[heads]).astype(
+                jnp.bfloat16
+            )
+            onward().start()
+
+    for part in range(2):
+        heads = pl.ds(part * half, half)
+
+        @pl.when(jnp.logical_not(last))
+        def _():
+            remote(
+                leaving.at[heads], arrived.at[heads], send.at[part], recv.at[part], *after
+            ).wait_send()
+
+
+def chain_states(fresh, keep, planes):
+    keep_rows = jnp.broadcast_to(keep[:, None, None], (keep.shape[0], 1, fresh.shape[2]))
+    dma = pltpu.SemaphoreType.DMA
+    return pl.pallas_call(
+        functools.partial(chain_kernel, planes),
+        out_shape=jax.ShapeDtypeStruct(fresh.shape, jnp.float32),
+        in_specs=[pl.BlockSpec(memory_space=pltpu.VMEM)] * 2,
+        out_specs=pl.BlockSpec(memory_space=pltpu.VMEM),
+        scratch_shapes=[
+            pltpu.VMEM(fresh.shape, jnp.bfloat16), pltpu.VMEM(fresh.shape, jnp.bfloat16),
+            dma((2,)), dma((2,)),
+        ],
+        compiler_params=pltpu.CompilerParams(
+            collective_id=1, has_side_effects=True, vmem_limit_bytes=16 << 20
+        ),
+        name="chain_states",
+    )(fresh, keep_rows)
+
+
+def tail_kernel(
+    inner_total, start, gated_ref, gain_ref, all_ref, out_ref,
+    weight, leaving, arrived, sq_leaving, sq_arrived, load, send, recv, sq_send, sq_recv,
+):
+    seq, tp, z, x, y, c = place()
+    share = 2 * y + x
+    width = gated_ref.shape[1]
+    fetch = pltpu.make_async_copy(all_ref.at[:, :, pl.ds(start, width)], weight, load.at[0])
+    fetch.start()
+    greet_plane(1)
+    gated = gated_ref[...]
+    sums = lax.dot_general(
+        jnp.ones((8, width), jnp.float32), gated * gated, (((1,), (1,)), ((), ())),
+        precision=HIGHEST_PREC, preferred_element_type=jnp.float32,
+    )
+    sq_leaving[...] = sums
+    scaled = (gated * gain_ref[...]).astype(jnp.bfloat16)
+    fetch.wait()
+    columns = 2 * weight.shape[1]
+
+    def outward(to):
+        return remote(leaving.at[to], arrived.at[share], send.at[to], recv.at[share], 2 * z + c, to)
+
+    def squares(to):
+        return remote(
+            sq_leaving, sq_arrived.at[share], sq_send.at[to], sq_recv.at[share], 2 * z + c, to
+        )
+
+    for to in range(4):
+        block = weight[2 * to : 2 * to + 2].reshape(columns, width)
+        product = lax.dot_general(
+            scaled, block, (((1,), (1,)), ((), ())), preferred_element_type=jnp.float32
+        ).astype(jnp.bfloat16)
+        itself = (x == c) & (tp == to)
+
+        @pl.when(itself)
+        def _():
+            arrived[share] = product
+            sq_arrived[share] = sums
+
+        @pl.when(jnp.logical_not(itself))
+        def _():
+            leaving[to] = product
+            outward(to).start()
+            squares(to).start()
+
+    total, sq_total = 0.0, 0.0
+    for slot in range(4):
+        @pl.when(jnp.logical_not((x == c) & (share == slot)))
+        def _():
+            remote(
+                leaving.at[0], arrived.at[slot], send.at[0], recv.at[slot], seq, tp + 1 - 2 * c
+            ).wait_recv()
+            remote(
+                sq_leaving, sq_arrived.at[slot], sq_send.at[0], sq_recv.at[slot],
+                seq, tp + 1 - 2 * c,
+            ).wait_recv()
+
+        total = total + arrived[slot].astype(jnp.float32)
+        sq_total = sq_total + sq_arrived[slot]
+    scale = lax.rsqrt(sq_total[0:1] / inner_total + EPSILON)
+    scale_rows = jnp.transpose(jnp.broadcast_to(scale, (128, scale.shape[1])))[:, 0:1]
+    out_ref[...] = (total * scale_rows).astype(out_ref.dtype)
+
+    for to in range(4):
+        itself = (x == c) & (tp == to)
+
+        @pl.when(jnp.logical_not(itself))
+        def _():
+            outward(to).wait_send()
+            squares(to).wait_send()
+
+
+def finish(gated, gain, gathered, start, width_here, inner_total):
+    rows, width = gated.shape
+    blocks, depth = gathered.shape[:2]
+    dma = pltpu.SemaphoreType.DMA
+    return pl.pallas_call(
+        functools.partial(tail_kernel, inner_total, start),
+        out_shape=jax.ShapeDtypeStruct((rows, width_here), jnp.bfloat16),
+        in_specs=[
+            pl.BlockSpec(memory_space=pltpu.VMEM),
+            pl.BlockSpec(memory_space=pltpu.VMEM),
+            pl.BlockSpec(memory_space=pl.ANY),
+        ],
+        out_specs=pl.BlockSpec(memory_space=pltpu.VMEM),
+        scratch_shapes=[
+            pltpu.VMEM((blocks, depth, width), jnp.bfloat16),
+            pltpu.VMEM((4, rows, width_here), jnp.bfloat16),
+            pltpu.VMEM((4, rows, width_here), jnp.bfloat16),
+            pltpu.VMEM((8, rows), jnp.float32),
+            pltpu.VMEM((4, 8, rows), jnp.float32),
+            dma((1,)), dma((4,)), dma((4,)), dma((4,)), dma((4,)),
+        ],
+        compiler_params=pltpu.CompilerParams(
+            collective_id=2, has_side_effects=True, vmem_limit_bytes=32 << 20
+        ),
+        name="project_out",
+    )(gated, gain, gathered)
+
+
+def on_device_paired(
+    hidden_in,
+    w_in_gate,
+    w_in_value,
+    w_in_shared,
+    w_in_step,
+    conv_value,
+    conv_shared,
+    dt_bias,
+    a_log,
+    skip_gain,
+    norm_gain,
+    w_out,
+    prompt_lengths,
+    row_blocks,
+):
+    seq_count = lax.axis_size("seq")
+    planes = seq_count // 2
+    here = 2 * (lax.axis_index("seq") // 2) + lax.axis_index("tp") % 2
+    tokens_here = hidden_in.shape[0]
+    edge_count = conv_value.shape[0] - 1
+    local_inner = conv_value.shape[1]
+    local_heads = dt_bias.shape[0]
+    shared_width = conv_shared.shape[1]
+    head_dim = local_inner // local_heads
+    state_size = shared_width // 2
+    rows_here = w_in_gate.shape[0]
+    step_width = 128
+    packed = jnp.concatenate(
+        [
+            w_in_value.astype(jnp.bfloat16),
+            w_in_shared.astype(jnp.bfloat16),
+            w_in_gate.astype(jnp.bfloat16),
+            jnp.pad(w_in_step.astype(jnp.bfloat16), ((0, 0), (0, step_width - local_heads))),
+            w_out.astype(jnp.bfloat16).T,
+        ],
+        axis=1,
+    )
+    scalars = jnp.pad(
+        jnp.concatenate([dt_bias, a_log, skip_gain]), (0, local_inner - 3 * local_heads)
+    )
+    spare = jnp.zeros((8 - edge_count - 3, local_inner), jnp.float32)
+    params = jnp.concatenate([conv_value, norm_gain[None], scalars[None], spare], axis=0)
+    features, gathered, params = gather_all(hidden_in, packed, params, planes)
+    taps_value = params[: edge_count + 1]
+    norm_gain = params[edge_count + 1]
+    scalars = params[edge_count + 2]
+    dt_bias = scalars[:local_heads]
+    a_log = scalars[local_heads : 2 * local_heads]
+    skip_gain = scalars[2 * local_heads : 3 * local_heads]
+
+    model_width = features.shape[0] * features.shape[2]
+    by_block = jnp.transpose(features, (1, 0, 2)).reshape(
+        tokens_here, seq_count, model_width // seq_count
+    )
+    permuted = jnp.take(by_block, row_blocks, axis=1).reshape(tokens_here, model_width)
+    in_width = 2 * local_inner + shared_width + step_width
+    projected = jnp.dot(
+        permuted,
+        gathered[:, :, :in_width].reshape(model_width, in_width),
+        preferred_element_type=jnp.float32,
+    ).astype(jnp.bfloat16)
+    mix_width = local_inner + shared_width
+    mixed_in = projected[:, :mix_width]
+    gate_all = projected[:, mix_width : mix_width + local_inner]
+    raw_all = projected[:, mix_width + local_inner : mix_width + local_inner + local_heads]
+
+    tp_count = lax.axis_size("tp")
+
+    def device(block, share):
+        z, c, y, x = block // 2, block % 2, share // 2, share % 2
+        return (2 * z + x) * tp_count + 2 * y + c
+
+    route = [
+        (device(block, share), device(block + 1, share))
+        for block in range(seq_count - 1)
+        for share in range(tp_count)
+    ]
+    edge_mix = lax.ppermute(mixed_in[tokens_here - edge_count :], ("seq", "tp"), route)
+    doc_ends = jnp.cumsum(prompt_lengths)
+    first_pos = here * tokens_here
+    positions = first_pos + jnp.arange(tokens_here, dtype=jnp.int32)
+    edge_positions = first_pos - edge_count + jnp.arange(edge_count, dtype=jnp.int32)
+    segments = segment_of(positions, doc_ends)
+    ext_segments = jnp.concatenate([segment_of(edge_positions, doc_ends), segments])
+    ext_rows = jnp.concatenate([edge_mix, mixed_in], axis=0)
+    kernel = jnp.concatenate([taps_value, conv_shared], axis=1)
+    conv_sum = jnp.zeros(mixed_in.shape, jnp.float32)
+    for tap_index in range(edge_count + 1):
+        same_doc = (ext_segments[tap_index : tap_index + tokens_here] == segments)[:, None]
+        conv_sum = conv_sum + jnp.where(
+            same_doc,
+            kernel[tap_index][None, :]
+            * ext_rows[tap_index : tap_index + tokens_here].astype(jnp.float32),
+            0.0,
+        )
+    convolved = jax.nn.silu(conv_sum).astype(jnp.bfloat16)
+    values = (
+        convolved[:, :local_inner].astype(jnp.float32).reshape(tokens_here, local_heads, head_dim)
+    )
+    b_half = convolved[:, local_inner : local_inner + state_size]
+    c_half = convolved[:, local_inner + state_size :]
+    c_rows = c_half.astype(jnp.float32)
+    steps_dt = jax.nn.softplus(raw_all.astype(jnp.float32) + dt_bias[None, :])
+    decay_rates = jnp.exp(a_log)
+    prev_first = segment_of(jnp.reshape(first_pos - 1, (1,)), doc_ends)[0]
+    parts = span_parts(values, b_half, c_half, steps_dt, decay_rates, segments, prev_first)
+    carried = chain_states(parts[2], parts[3], planes)
+    intra_part, carry_in, _, _ = parts
+    inter_part = (
+        jnp.einsum("in,hpn->ihp", c_rows, carried, precision=HIGHEST_PREC) * carry_in[:, :, None]
+    )
+    outputs = intra_part + inter_part
+    mixed_heads = outputs + skip_gain[None, :, None] * values
+    gated = mixed_heads.reshape(tokens_here, local_inner) * jax.nn.silu(
+        gate_all.astype(jnp.float32)
+    )
+    return finish(
+        gated,
+        norm_gain[None],
+        gathered,
+        in_width,
+        hidden_in.shape[1],
+        local_inner * tp_count,
+    )
+
+
+def paired(mesh):
+    return dict(mesh.shape) == {"seq": 8, "tp": 4}
+
+
 def solution(mesh):
     return jax.shard_map(
-        on_device,
+        on_device_paired if paired(mesh) else on_device_plain,
         mesh=mesh,
         in_specs=(
             P("seq", "tp"),

time: 290 us -> 146 us (0.50)
  waiting for transfers between devices: 143 us -> 0.01 us
  Pallas kernels: 0 us -> 112 us
  blocking collectives: 80.6 us -> 0 us
  between operations: 14.7 us -> 1.54 us
  other arithmetic: 20.2 us -> 12.5 us
  matrix products: 14.9 us -> 8.4 us
  starting transfers between devices: 5.72 us -> 1.29 us
    all_gather x4 -> x0, waiting for transfers between devices: 120 us -> none  [the longest x1 44.2 us: on_device(): lax.all_gather(out_weight, 'seq', axis=1, tiled=True)]
    pallas_call x0 -> x3, Pallas kernels: none -> 112 us  [the longest x1 81.2 us: gather_all(): pl.pallas_call(functools.partial(gather_kernel, planes), out_shape=(jax.S...]
    all_gather x4 -> x0, blocking collectives: 74.8 us -> none  [the longest x1 26.2 us: on_device(): lax.all_gather(stored[2], 'seq', axis=0, tiled=True)]
    unnamed x6 -> x0, waiting for transfers between devices: 22.6 us -> none
    select_n x11 -> x2, other arithmetic: 9.43 us -> 0.66 us  [the longest x1 0.66 us: on_device_paired(): jnp.take(by_block, row_blocks, axis=1).reshape(tokens_here, model_width)]
    psum x1 -> x0, blocking collectives: 5.77 us -> none  [on_device(): square_total = lax.psum(squares, 'tp')]
    dot_general x6 -> x2, matrix products: 9.91 us -> 5.1 us  [the longest x1 4.58 us: on_device_paired(): jnp.dot(permuted, gathered[:, :, :in_width].reshape(model_width, in_width...]
    ppermute x1, starting transfers between devices: 5.55 us -> 1.29 us  [on_device_paired(): lax.ppermute(mixed_in[tokens_here - edge_count:], ('seq', 'tp'), route)]
  transfers between devices with their start and end apart: 6 -> 1, of which waited for: 5 -> 0; matrix products, arithmetic and copies ran while one was open for 10% -> 3% of each run, Pallas kernels for 0% -> 0%
where the time goes in v1:
time: 146 us; the launch traced here: 145 us
  Pallas kernels  112 us (77%)
  other arithmetic  12.5 us (9%)
  local copies, waits for them, and re-layouts  9.14 us (6%)
  matrix products  8.4 us (6%)
  between operations  1.54 us (1%)
    pallas_call x1, Pallas kernels, gather_all(): pl.pallas_call(functools.partial(gather_kernel, planes), out_shape=(jax.S...  81.2 us
    pallas_call x1, Pallas kernels, finish(): pl.pallas_call(functools.partial(tail_kernel, inner_total, start), out_sh...  15.6 us
    pallas_call x1, Pallas kernels, chain_states(): pl.pallas_call(functools.partial(chain_kernel, planes), out_shape=jax.Sha...  15.4 us
    dot_general x1, matrix products, on_device_paired(): jnp.dot(permuted, gathered[:, :, :in_width].reshape(model_width, in_width...  4.58 us
    unnamed x14, local copies, waits for them, and re-layouts  4.27 us
    unnamed x3, other arithmetic  3.13 us
  transfers between devices with their start and end apart: 1, of which 0 were waited for; matrix products, arithmetic and copies ran while one was open for 3% of the time, Pallas kernels for 0%

profile of v1, /device:TPU:29, one launch (start us, length us, event | category | flops | bytes accessed | tf_op | source)
XLA Modules:
  0.0 145.0 jit_solution(2776281411481285898)
XLA Ops:
  0.0 0.7 compare_and_fusion
  0.7 0.7 compare_select_fusion.1
  1.3 0.7 broadcast_in_dim.117
  2.0 0.8 select_maximum_fusion
  2.8 0.7 convert_element_type.69
  3.7 1.1 convert_dynamic-update-slice_fusion.1
  4.8 0.9 convert_dynamic-update-slice_fusion.2
  5.8 1.1 convert_dynamic-update-slice_fusion
  6.9 1.1 bitcast_dynamic-update-slice_fusion.w_ref
  8.0 0.8 maximum_maximum_fusion.p_ref
  9.1 81.2 %gather_weights.1 = (bf16[4,256,384]{2,1,0:T(8,128)(2,1)}, bf16[8,192,2688]{2,1,0:T(8,128)(2,1)}, f32[8,768]{1,0:T(8,128)}) custom-call(bf16[256,384]{1,0:T(8,128)(2,1)} %h_ref.1, bf16[192,2688]{1,0:T(8,128)(2,1)} %copy-done.1, f32[8,768]{1,0:T(8,128)} %maximum_maximum_fusion.p_ref), custom_call_target="tpu_custom_call" | custom-call | tf_op jit(solution)/shard_map/gather_weights/pallas_call | solution.py:362
  90.3 1.4 copy.49
  91.7 0.6 gather_fusion
  92.3 4.6 %fusion.12 = bf16[256,1920]{1,0:T(8,128)(2,1)S(1)} fusion(bf16[8,192,2688]{2,1,0:T(8,128)(2,1)} %get-tuple-element.10.all_ref, bf16[8,256,192]{1,2,0:T(8,128)(2,1)S(1)} %gather_fusion, pred[8]{0:T(512)(128)(4,1)S(1)} %compare_and_fusion), kind=kOutput, calls=%fused_computation.11 | convolution fusion | flops 1510834176 | bytes 7667720 | tf_op jit(solution)/shard_map/dot_general | solution.py:610
  96.9 1.3 collective-permute-start
  99.3 0.6 fusion.49
  101.4 1.3 broadcast_compare_fusion
  102.9 0.6 reduce-window.11
  104.5 0.8 multiply_convert_fusion
  106.4 15.4 %chain_states.1 = f32[12,64,128]{2,1,0:T(8,128)S(1)} custom-call(f32[12,64,128]{2,1,0:T(8,128)S(1)} %fusion.26.fresh_ref, f32[12,1,128]{2,1,0:T(1,128)S(1)} %broadcast_in_dim.130.keep_ref), custom_call_target="tpu_custom_call" | custom-call | tf_op jit(solution)/shard_map/chain_states/pallas_call | solution.py:436
  121.8 2.6 %fusion.21 = f32[256,12,64]{0,2,1:T(8,128)S(1)} fusion(bf16[256,12,64]{0,2,1:T(8,128)(2,1)S(1)} %bitcast.50, f32[256,12]{0,1:T(8,128)S(1)} %copy.55, f32[256,12]{0,1:T(8,128)S(1)} %copy.53, f32[256,256]{1,0:T(8,128)S(1)} %fusion.42, pred[256,256]{1,0:T(8,128)(4,1)S(1)} %fusion.38), kind=kOutput, calls=%fused_computation.18 | convolution fusion | flops 607911936 | bytes 1531904 | tf_op jit(solution)/shard_map/ijh,jhp->ihp/dot_general | solution.py:56
  125.4 3.3 %copy-done = bf16[8,192,2688]{2,1,0:T(8,128)(2,1)S(1)} copy-done((bf16[8,192,2688]{2,1,0:T(8,128)(2,1)S(1)}, bf16[8,192,2688]{2,1,0:T(8,128)(2,1)}, u32[]{:S(2)}) %copy-start) | copy-done | bytes 8257560
  128.7 15.6 %project_out.1 = bf16[256,384]{1,0:T(8,128)(2,1)S(1)} custom-call(f32[256,768]{1,0:T(8,128)S(1)} %fusion.30.gated_ref, f32[1,768]{1,0:T(1,128)S(1)} %slice.117.gain_ref, bf16[8,192,2688]{2,1,0:T(8,128)(2,1)S(1)} %copy-done), custom_call_target="tpu_custom_call" | custom-call | tf_op jit(solution)/shard_map/project_out/pallas_call | solution.py:529
  144.3 0.7 copy.64
  (54 shorter events, 4.9 us)
Async XLA Ops:
  0.0 8.0 %copy-start.2 = (f32[4,768]{1,0:T(4,128)S(1)}, f32[4,768]{1,0:T(4,128)}, u32[]{:S(2)}) copy-start(f32[4,768]{1,0:T(4,128)} %param.19) | copy-start | bytes 36868
  8.0 1.1 copy-start.1
  92.3 6.0 %copy-start.5 = (s32[8]{0:T(128)S(1)}, s32[8]{0:T(128)}, u32[]{:S(2)}) copy-start(s32[8]{0:T(128)} %param.26) | copy-start | bytes 100
  92.3 6.9 %copy-start.3 = (f32[8,768]{1,0:T(8,128)S(1)}, f32[8,768]{1,0:T(8,128)}, u32[]{:S(2)}) copy-start(f32[8,768]{1,0:T(8,128)} %get-tuple-element.8) | copy-start | bytes 73732
  92.3 11.7 %copy-start.4 = (f32[4,256]{1,0:T(4,128)S(1)}, f32[4,256]{1,0:T(4,128)}, u32[]{:S(2)}) copy-start(f32[4,256]{1,0:T(4,128)} %param.20) | copy-start | bytes 12292
  96.9 7.6 %collective-permute-start = (bf16[3,1024]{1,0:T(4,128)(2,1)S(1)}, bf16[3,1024]{1,0:T(4,128)(2,1)S(1)}, u32[]{:S(2)}, u32[]{:S(2)}) collective-permute-start(bf16[3,1024]{1,0:T(4,128)(2,1)S(1)} %slice.122), channel_id=1, source_target_pairs={{0,1},{4,5},{2,3},{6,7},{1,8},{5,12},{3,10},{7,14},{8,9},{12,13},{... | collective-permute-start | bytes 18440 | tf_op jit(solution)/shard_map/ppermute | solution.py:631
  125.4 3.3 %copy-start = (bf16[8,192,2688]{2,1,0:T(8,128)(2,1)S(1)}, bf16[8,192,2688]{2,1,0:T(8,128)(2,1)}, u32[]{:S(2)}) copy-start(bf16[8,192,2688]{2,1,0:T(8,128)(2,1)} %get-tuple-element.10.all_ref) | copy-start | bytes 24772612

commit v2 on v0

--- a/solution.py
+++ b/solution.py
@@ -1,7 +1,13 @@
+import functools
+
 import jax
 import jax.numpy as jnp
 from jax import lax
+from jax.experimental import pallas as pl
+from jax.experimental.pallas import tpu as pltpu
 from jax.sharding import PartitionSpec as P
+
+MESH = pl.DeviceIdType.MESH
 
 EPSILON = 1e-05
 HIGHEST_PREC = lax.Precision.HIGHEST
@@ -63,7 +69,7 @@
     return (earlier[0] * later[0], later[0][:, None, None] * earlier[1] + later[1])
 
 
-def on_device(
+def on_device_plain(
     hidden_in,
     w_in_gate,
     w_in_value,
@@ -174,9 +180,570 @@
     )
 
 
+def place():
+    seq, tp = lax.axis_index("seq"), lax.axis_index("tp")
+    return seq, tp, seq // 2, seq % 2, tp // 2, tp % 2
+
+
+def remote(src, dst, send, recv, seq, tp):
+    return pltpu.make_async_remote_copy(
+        src_ref=src, dst_ref=dst, send_sem=send, recv_sem=recv,
+        device_id=(seq, tp), device_id_type=MESH,
+    )
+
+
+def greet(planes):
+    seq, tp, z, x, y, c = place()
+    barrier = pltpu.get_barrier_semaphore()
+
+    def meet(to_seq, to_tp):
+        pl.semaphore_signal(barrier, inc=1, device_id=(to_seq, to_tp), device_id_type=MESH)
+
+    for other in range(1, 8):
+        dx, dt = other // 4, other % 4
+        meet(2 * z + (x + dx) % 2, (tp + dt) % 4)
+
+    @pl.when(z > 0)
+    def _():
+        meet(seq - 2, tp)
+
+        @pl.when(c == 0)
+        def _():
+            meet(seq - 2, tp + 1)
+
+    @pl.when(z < planes - 1)
+    def _():
+        meet(seq + 2, tp)
+
+        @pl.when(c == 1)
+        def _():
+            meet(seq + 2, tp - 1)
+
+    below = jnp.where(z > 0, 2 - c, 0)
+    above = jnp.where(z < planes - 1, 1 + c, 0)
+    pl.semaphore_wait(barrier, 7 + below + above)
+
+
+class Relay:
+    def __init__(self, planes, depth, own, every, sems):
+        self.planes, self.depth, self.own, self.every = planes, depth, own, every
+        self.got, self.swapped, self.up, self.down, self.across = sems
+        self.chunks = own.shape[0] // depth
+        self.at = place()
+
+    def rows(self, k):
+        return pl.ds(pl.multiple_of(k * self.depth, self.depth), self.depth)
+
+    def local(self, k):
+        seq, tp, z, x, y, c = self.at
+        return pltpu.make_async_copy(
+            self.own.at[self.rows(k)], self.every.at[2 * z + c, self.rows(k)], self.got.at[2 * z + c, k]
+        )
+
+    def swap(self, k):
+        seq, tp, z, x, y, c = self.at
+        slot = 2 * z + 1 - c
+        return remote(
+            self.own.at[self.rows(k)], self.every.at[slot, self.rows(k)],
+            self.swapped.at[k], self.got.at[slot, k], seq + 1 - 2 * x, tp + 1 - 2 * c,
+        )
+
+    def sent(self, slot, k, sems, to_seq, to_tp):
+        here = self.every.at[slot, self.rows(k)]
+        return remote(here, here, sems.at[slot // 2, k], self.got.at[slot, k], to_seq, to_tp)
+
+    def going_up(self, slot, k):
+        return self.sent(slot, k, self.up, self.at[0] + 2, self.at[1])
+
+    def going_down(self, slot, k):
+        return self.sent(slot, k, self.down, self.at[0] - 2, self.at[1])
+
+    def going_across(self, slot, k):
+        return self.sent(slot, k, self.across, self.at[0], self.at[1] + 1 - 2 * self.at[5])
+
+    def start(self):
+        seq, tp, z, x, y, c = self.at
+
+        @pl.when(x == c)
+        def _():
+            @pl.loop(0, self.chunks)
+            def _(k):
+                self.local(k).start()
+
+        @pl.when(x != c)
+        def _():
+            @pl.loop(0, self.chunks)
+            def _(k):
+                self.swap(k).start()
+
+    def turn(self, far):
+        seq, tp, z, x, y, c = self.at
+        mine = 2 * z + c
+
+        @pl.loop(0, self.chunks)
+        def _(k):
+            if far == 0:
+                @pl.when(x == c)
+                def _():
+                    self.local(k).wait()
+
+                @pl.when(x != c)
+                def _():
+                    self.going_across(mine, k).wait_recv()
+
+                @pl.when(z < self.planes - 1)
+                def _():
+                    self.going_up(mine, k).start()
+
+                @pl.when(z > 0)
+                def _():
+                    self.going_down(mine, k).start()
+
+                self.going_across(mine, k).start()
+            else:
+                @pl.when(z >= far)
+                def _():
+                    slot = mine - 2 * far
+                    self.going_across(slot, k).wait_recv()
+
+                    @pl.when(z < self.planes - 1)
+                    def _():
+                        self.going_up(slot, k).start()
+
+                    self.going_across(slot, k).start()
+
+                @pl.when(z < self.planes - far)
+                def _():
+                    slot = mine + 2 * far
+                    self.going_across(slot, k).wait_recv()
+
+                    @pl.when(z > 0)
+                    def _():
+                        self.going_down(slot, k).start()
+
+                    self.going_across(slot, k).start()
+
+    def arrive(self):
+        c = self.at[5]
+
+        @pl.loop(0, self.chunks)
+        def _(k):
+            for at in range(self.planes):
+                self.going_across(2 * at + 1 - c, k).wait_recv()
+
+    def leave(self):
+        seq, tp, z, x, y, c = self.at
+
+        @pl.loop(0, self.chunks)
+        def _(k):
+            for at in range(self.planes):
+                slot = 2 * at + c
+                self.going_across(slot, k).wait_send()
+
+                @pl.when((z < self.planes - 1) & (z >= at))
+                def _():
+                    self.going_up(slot, k).wait_send()
+
+                @pl.when((z > 0) & (z <= at))
+                def _():
+                    self.going_down(slot, k).wait_send()
+
+            @pl.when(x != c)
+            def _():
+                self.swap(k).wait_send()
+
+
+def mixer_kernel(
+    planes, heads, inner_total,
+    lengths_ref, order_ref, h_ref, gate_ref, value_ref, shared_ref, step_ref, taps_ref,
+    shared_taps_ref, bias_ref, log_ref, skip_ref, gain_ref, w_out_ref, out_ref,
+    w_own, w_all, o_all, h_own, h_all, p_own, par, gates, rows_ext, edge_own, edge_got, mixed,
+    fresh, state_got, state_own, leaving, arrived, sq_leaving, sq_arrived,
+    w_got, w_swapped, w_up, w_down, w_across, o_got, o_swapped, o_up, o_down, o_across,
+    h_send, h_got, p_sems, edge_sems, state_sems, send, recv, sq_send, sq_recv,
+):
+    f32, bf16 = jnp.float32, jnp.bfloat16
+    seq, tp, z, x, y, c = place()
+    share = 2 * y + x
+    first, last = (z == 0) & (c == 0), (z == planes - 1) & (c == 1)
+    before = (seq - 2 * (1 - c), tp + 1 - 2 * c)
+    after = (seq + 2 * c, tp + 1 - 2 * c)
+    tokens, width = h_ref.shape[0], value_ref.shape[1]
+    shared_width = shared_ref.shape[1]
+    mix_width, state_size, head_dim = width + shared_width, shared_width // 2, width // heads
+    half_features = h_ref.shape[1] // 2
+    step_at = mix_width + width
+
+    w_own[:, 0:width] = value_ref[...].astype(bf16)
+    w_own[:, width:mix_width] = shared_ref[...].astype(bf16)
+    w_own[:, mix_width:step_at] = gate_ref[...].astype(bf16)
+    w_own[:, step_at:] = jnp.zeros((w_own.shape[0], w_own.shape[1] - step_at), bf16)
+    w_own[:, step_at : step_at + heads] = step_ref[...].astype(bf16)
+    h_own[0] = h_ref[:, 0:half_features]
+    h_own[1] = h_ref[:, half_features:]
+    p_own[...] = jnp.zeros_like(p_own)
+    p_own[0:4, :] = taps_ref[...]
+    p_own[4:5, :] = gain_ref[...]
+    p_own[5:6, 0:heads] = bias_ref[...]
+    p_own[6:7, 0:heads] = log_ref[...]
+    p_own[7:8, 0:heads] = skip_ref[...]
+    greet(planes)
+
+    into = Relay(planes, 48, w_own, w_all, (w_got, w_swapped, w_up, w_down, w_across))
+    out_of = Relay(planes, 96, w_out_ref, o_all, (o_got, o_swapped, o_up, o_down, o_across))
+    par_local = pltpu.make_async_copy(p_own, par, p_sems.at[0])
+    par_swap = remote(p_own, par, p_sems.at[1], p_sems.at[0], seq + 1 - 2 * x, tp + 1 - 2 * c)
+    into.start()
+
+    def features(to):
+        return remote(
+            h_own, h_all.at[pl.ds(2 * tp, 2)], h_send.at[to], h_got.at[tp],
+            2 * z + to // 2, 2 * (to % 2) + x,
+        )
+
+    own_features = pltpu.make_async_copy(h_own, h_all.at[pl.ds(2 * tp, 2)], h_got.at[tp])
+    for to in range(4):
+        itself = (x == c) & (x == to // 2) & (y == to % 2)
+
+        @pl.when(itself)
+        def _():
+            own_features.start()
+
+        @pl.when(jnp.logical_not(itself))
+        def _():
+            features(to).start()
+
+    @pl.when(x == c)
+    def _():
+        par_local.start()
+
+    @pl.when(x != c)
+    def _():
+        par_swap.start()
+
+    into.turn(0)
+    out_of.start()
+    for far in range(1, planes):
+        into.turn(far)
+    out_of.turn(0)
+
+    for quarter in range(4):
+        remote(
+            h_own, h_all.at[pl.ds(2 * quarter, 2)], h_send.at[0], h_got.at[quarter],
+            seq, tp + 1 - 2 * c,
+        ).wait_recv()
+
+    @pl.when(x == c)
+    def _():
+        par_local.wait()
+
+    @pl.when(x != c)
+    def _():
+        par_swap.wait()
+
+    into.arrive()
+
+    def project(start, size):
+        total = jnp.zeros((tokens, size), f32)
+        for block in range(2 * planes):
+            total = total + jnp.dot(
+                h_all[order_ref[block]], w_all[block, :, start : start + size],
+                preferred_element_type=f32,
+            )
+        return total.astype(bf16)
+
+    for part in range(0, mix_width, 512):
+        done = project(part, 512)
+        rows_ext[8:, part : part + 512] = done.astype(f32)
+        edge_own[:, part : part + 512] = done[tokens - 16 :]
+
+    def edge(to):
+        return remote(edge_own, edge_got, edge_sems.at[0], edge_sems.at[1], *to)
+
+    @pl.when(jnp.logical_not(last))
+    def _():
+        edge(after).start()
+
+    gates[...] = project(mix_width, width)
+    raw = project(step_at, w_own.shape[1] - step_at).astype(f32)
+
+    lane_heads = lax.broadcasted_iota(jnp.int32, (1, 128), 1) < heads
+    bias = jnp.where(lane_heads, par[5:6, 0:128], 0.0)
+    rate = jnp.where(lane_heads, jnp.exp(par[6:7, 0:128]), 0.0)
+    shifted = raw + bias
+    dt = jnp.maximum(shifted, 0.0) + jnp.log1p(jnp.exp(-jnp.abs(shifted)))
+    row_at = lax.broadcasted_iota(jnp.int32, (tokens, tokens), 0)
+    column_at = lax.broadcasted_iota(jnp.int32, (tokens, tokens), 1)
+    first_pos = (2 * z + c) * tokens
+    ends = [lengths_ref[0]]
+    for i in range(1, lengths_ref.shape[0]):
+        ends.append(ends[-1] + lengths_ref[i])
+
+    def segment(position):
+        count = jnp.zeros_like(position)
+        for end in ends:
+            count = count + (position >= end).astype(jnp.int32)
+        return count
+
+    row_segments, column_segments = segment(first_pos + row_at), segment(first_pos + column_at)
+    causal = (row_at >= column_at) & (row_segments == column_segments)
+    lower = (row_at >= column_at).astype(f32)
+    summed = jnp.dot(lower, -dt * rate, precision=HIGHEST_PREC, preferred_element_type=f32)
+    summed_rows, dt_rows = jnp.transpose(summed), jnp.transpose(dt)
+    positions = first_pos + lax.broadcasted_iota(jnp.int32, (tokens, 128), 0)
+    segments = segment(positions)
+    prev_segment = segment(jnp.full((tokens, 128), first_pos - 1, jnp.int32))
+    last_segment = segment(jnp.full((tokens, 128), first_pos + tokens - 1, jnp.int32))
+    carry_in = jnp.where(segments == prev_segment, jnp.exp(summed), 0.0)
+    end_sum = summed[tokens - 1 : tokens]
+    tail = jnp.where(segments == last_segment, jnp.exp(end_sum - summed), 0.0) * dt
+    keep = jnp.where(last_segment[0:8] == prev_segment[0:8], jnp.exp(end_sum), 0.0)
+    spread = (
+        lax.broadcasted_iota(jnp.int32, (128, width), 1) // head_dim
+        == lax.broadcasted_iota(jnp.int32, (128, width), 0)
+    ).astype(f32)
+
+    def over_channels(per_head):
+        return jnp.dot(per_head, spread, precision=HIGHEST_PREC, preferred_element_type=f32)
+
+    keep_rows = lax.dot_general(
+        spread, keep, (((0,), (1,)), ((), ())), precision=HIGHEST_PREC, preferred_element_type=f32
+    )[:, 0:1]
+
+    @pl.when(first)
+    def _():
+        rows_ext[0:8] = jnp.zeros((8, mix_width), f32)
+
+    @pl.when(jnp.logical_not(first))
+    def _():
+        edge(before).wait_recv()
+        rows_ext[0:8] = edge_got[...].astype(f32)[8:16]
+
+    def convolve(start, size, taps):
+        total = jnp.zeros((tokens, size), f32)
+        for k in range(4):
+            back = 3 - k
+            counted = (segment(positions - back) == segments) & (positions >= back)
+            term = taps[k : k + 1] * rows_ext[8 - back : 8 - back + tokens, start : start + size]
+            total = total + jnp.where(counted[:, 0:1], term, 0.0)
+        return jax.nn.silu(total).astype(bf16)
+
+    mixed[:, 0:width] = convolve(0, width, par[0:4])
+    mixed[:, width:] = convolve(width, shared_width, shared_taps_ref[...])
+    values = mixed[:, 0:width]
+    b_rows = mixed[:, width : width + state_size]
+    c_rows = mixed[:, width + state_size :]
+    weighted = (values.astype(f32) * over_channels(tail)).astype(bf16)
+    fresh[...] = lax.dot_general(
+        weighted, b_rows, (((0,), (0,)), ((), ())), preferred_element_type=f32
+    )
+
+    def state(to):
+        return remote(state_own, state_got, state_sems.at[0], state_sems.at[1], *to)
+
+    @pl.when(first)
+    def _():
+        state_got[...] = jnp.zeros_like(state_got)
+        state_own[...] = fresh[...].astype(bf16)
+        state(after).start()
+
+    out_of.turn(1)
+    scores = lax.dot_general(c_rows, b_rows, (((1,), (1,)), ((), ())), preferred_element_type=f32)
+    scores = jnp.where(causal, scores, 0.0)
+    for head in range(heads):
+        gap = summed[:, head : head + 1] - summed_rows[head : head + 1]
+        weights = scores * jnp.exp(jnp.where(causal, gap, 0.0)) * dt_rows[head : head + 1]
+        at = slice(head * head_dim, (head + 1) * head_dim)
+        rows_ext[8:, at] = jnp.dot(
+            weights.astype(bf16), mixed[:, at], preferred_element_type=f32
+        )
+
+    @pl.when(jnp.logical_not(first))
+    def _():
+        state(before).wait_recv()
+
+        @pl.when(jnp.logical_not(last))
+        def _():
+            state_own[...] = (keep_rows * state_got[...].astype(f32) + fresh[...]).astype(bf16)
+            state(after).start()
+
+    for far in range(2, planes):
+        out_of.turn(far)
+    inter = lax.dot_general(
+        c_rows, state_got[...], (((1,), (1,)), ((), ())), preferred_element_type=f32
+    ) * over_channels(carry_in)
+    skip = over_channels(
+        jnp.broadcast_to(jnp.where(lane_heads, par[7:8, 0:128], 0.0), (8, 128))
+    )[0:1]
+    gated = (rows_ext[8:, 0:width] + inter + skip * values.astype(f32)) * jax.nn.silu(
+        gates[...].astype(f32)
+    )
+    sums = lax.dot_general(
+        jnp.ones((8, width), f32), gated * gated, (((1,), (1,)), ((), ())),
+        precision=HIGHEST_PREC, preferred_element_type=f32,
+    )
+    sq_leaving[...] = sums
+    scaled = (gated * par[4:5]).astype(bf16)
+    out_of.arrive()
+    columns = 2 * w_out_ref.shape[0]
+
+    def outward(to):
+        return remote(leaving.at[to], arrived.at[share], send.at[to], recv.at[share], 2 * z + c, to)
+
+    def squares(to):
+        return remote(
+            sq_leaving, sq_arrived.at[share], sq_send.at[to], sq_recv.at[share], 2 * z + c, to
+        )
+
+    for to in range(4):
+        product = lax.dot_general(
+            scaled, o_all[2 * to : 2 * to + 2].reshape(columns, width),
+            (((1,), (1,)), ((), ())), preferred_element_type=f32,
+        ).astype(bf16)
+        itself = (x == c) & (tp == to)
+
+        @pl.when(itself)
+        def _():
+            arrived[share] = product
+            sq_arrived[share] = sums
+
+        @pl.when(jnp.logical_not(itself))
+        def _():
+            leaving[to] = product
+            outward(to).start()
+            squares(to).start()
+
+    into.leave()
+    out_of.leave()
+    for to in range(4):
+        itself = (x == c) & (x == to // 2) & (y == to % 2)
+
+        @pl.when(jnp.logical_not(itself))
+        def _():
+            features(to).wait_send()
+
+    @pl.when(jnp.logical_not(last))
+    def _():
+        edge(after).wait_send()
+        state(after).wait_send()
+
+    total, sq_total = 0.0, 0.0
+    for slot in range(4):
+        @pl.when(jnp.logical_not((x == c) & (share == slot)))
+        def _():
+            remote(
+                leaving.at[0], arrived.at[slot], send.at[0], recv.at[slot], seq, tp + 1 - 2 * c
+            ).wait_recv()
+            remote(
+                sq_leaving, sq_arrived.at[slot], sq_send.at[0], sq_recv.at[slot],
+                seq, tp + 1 - 2 * c,
+            ).wait_recv()
+
+        total = total + arrived[slot].astype(f32)
+        sq_total = sq_total + sq_arrived[slot]
+    scale = lax.rsqrt(sq_total[0:1] / inner_total + EPSILON)
+    scale_rows = jnp.transpose(jnp.broadcast_to(scale, (128, tokens)))[:, 0:1]
+    out_ref[...] = (total * scale_rows).astype(out_ref.dtype)
+
+    for to in range(4):
+        itself = (x == c) & (tp == to)
+
+        @pl.when(jnp.logical_not(itself))
+        def _():
+            outward(to).wait_send()
+            squares(to).wait_send()
+
+
+def on_device_paired(
+    hidden_in,
+    w_in_gate,
+    w_in_value,
+    w_in_shared,
+    w_in_step,
+    conv_value,
+    conv_shared,
+    dt_bias,
+    a_log,
+    skip_gain,
+    norm_gain,
+    w_out,
+    prompt_lengths,
+    row_blocks,
+):
+    blocks = lax.axis_size("seq")
+    planes = blocks // 2
+    tokens, features = hidden_in.shape
+    rows, width = w_in_value.shape
+    shared_width, heads = w_in_shared.shape[1], dt_bias.shape[0]
+    mix_width = width + shared_width
+    in_width = mix_width + width + 128
+    state_size = shared_width // 2
+    out_columns = w_out.shape[1]
+    f32, bf16, dma = jnp.float32, jnp.bfloat16, pltpu.SemaphoreType.DMA
+    vmem, smem = pl.BlockSpec(memory_space=pltpu.VMEM), pl.BlockSpec(memory_space=pltpu.SMEM)
+
+    def relay_sems(chunks):
+        return [dma((blocks, chunks)), dma((chunks,))] + [dma((planes, chunks))] * 3
+
+    return pl.pallas_call(
+        functools.partial(mixer_kernel, planes, heads, width * lax.axis_size("tp")),
+        out_shape=jax.ShapeDtypeStruct((tokens, features), bf16),
+        in_specs=[smem] * 2 + [vmem] * 12,
+        out_specs=vmem,
+        scratch_shapes=[
+            pltpu.VMEM((rows, in_width), bf16),
+            pltpu.VMEM((blocks, rows, in_width), bf16),
+            pltpu.VMEM((blocks, out_columns, width), bf16),
+            pltpu.VMEM((2, tokens, features // 2), bf16),
+            pltpu.VMEM((8, tokens, features // 2), bf16),
+            pltpu.VMEM((8, width), f32),
+            pltpu.VMEM((8, width), f32),
+            pltpu.VMEM((tokens, width), bf16),
+            pltpu.VMEM((tokens + 8, mix_width), f32),
+            pltpu.VMEM((16, mix_width), bf16),
+            pltpu.VMEM((16, mix_width), bf16),
+            pltpu.VMEM((tokens, mix_width), bf16),
+            pltpu.VMEM((width, state_size), f32),
+            pltpu.VMEM((width, state_size), bf16),
+            pltpu.VMEM((width, state_size), bf16),
+            pltpu.VMEM((4, tokens, features), bf16),
+            pltpu.VMEM((4, tokens, features), bf16),
+            pltpu.VMEM((8, tokens), f32),
+            pltpu.VMEM((4, 8, tokens), f32),
+        ]
+        + relay_sems(rows // 48)
+        + relay_sems(out_columns // 96)
+        + [dma((4,)), dma((4,)), dma((2,)), dma((2,)), dma((2,))]
+        + [dma((4,))] * 4,
+        compiler_params=pltpu.CompilerParams(
+            collective_id=0, has_side_effects=True, vmem_limit_bytes=50 << 20
+        ),
+        name="mixer",
+    )(
+        prompt_lengths,
+        row_blocks,
+        hidden_in,
+        w_in_gate,
+        w_in_value,
+        w_in_shared,
+        w_in_step,
+        conv_value,
+        conv_shared,
+        dt_bias[None],
+        a_log[None],
+        skip_gain[None],
+        norm_gain[None],
+        w_out.astype(bf16).T,
+    )
+
+
+def paired(mesh):
+    return dict(mesh.shape) == {"seq": 8, "tp": 4}
+
+
 def solution(mesh):
     return jax.shard_map(
-        on_device,
+        on_device_paired if paired(mesh) else on_device_plain,
         mesh=mesh,
         in_specs=(
             P("seq", "tp"),

time: 290 us -> 106 us (0.37)
  waiting for transfers between devices: 143 us -> 0 us
  Pallas kernels: 0 us -> 100 us
  blocking collectives: 80.6 us -> 0 us
  other arithmetic: 20.2 us -> 1.29 us
  matrix products: 14.9 us -> 0 us
  between operations: 14.7 us -> 0.17 us
  starting transfers between devices: 5.72 us -> 0 us
  local copies, waits for them, and re-layouts: 6.99 us -> 3.31 us
    all_gather x4 -> x0, waiting for transfers between devices: 120 us -> none  [the longest x1 44.2 us: on_device(): lax.all_gather(out_weight, 'seq', axis=1, tiled=True)]
    pallas_call x0 -> x1, Pallas kernels: none -> 100 us  [on_device_paired(): pl.pallas_call(functools.partial(mixer_kernel, planes, heads, width * lax...]
    all_gather x4 -> x0, blocking collectives: 74.8 us -> none  [the longest x1 26.2 us: on_device(): lax.all_gather(stored[2], 'seq', axis=0, tiled=True)]
    unnamed x6 -> x0, waiting for transfers between devices: 22.6 us -> none
    dot_general x9 -> x0, matrix products: 14.9 us -> none  [the longest x4 5.8 us: on_device(): jnp.dot(permuted, weight_piece, preferred_element_type=jnp.float32)]
    select_n x11 -> x0, other arithmetic: 9.43 us -> none  [the longest x8 8.41 us: turn(): return jax.tree.map(lambda a, b: jnp.where(reached, a, b), new, before)]
    psum x1 -> x0, blocking collectives: 5.77 us -> none  [on_device(): square_total = lax.psum(squares, 'tp')]
    ppermute x1 -> x0, starting transfers between devices: 5.55 us -> none  [passed_along(): return lax.ppermute(block, axis, route)]
  transfers between devices with their start and end apart: 6 -> 0, of which waited for: 5 -> 0; matrix products, arithmetic and copies ran while one was open for 10% -> 0% of each run, Pallas kernels for 0% -> 0%
where the time goes in v2:
time: 106 us; the launch traced here: 105 us
  Pallas kernels  100 us (94%)
  local copies, waits for them, and re-layouts  3.31 us (3%)
  other arithmetic  1.29 us (1%)
    pallas_call x1, Pallas kernels, on_device_paired(): pl.pallas_call(functools.partial(mixer_kernel, planes, heads, width * lax...  100 us
    unnamed x26, local copies, waits for them, and re-layouts  3.3 us

profile of v2, /device:TPU:29, one launch (start us, length us, event | category | flops | bytes accessed | tf_op | source)
XLA Modules:
  0.0 104.9 jit_solution(4038076016676170553)
XLA Ops:
  0.0 0.7 copy-done.11
  0.7 0.8 copy.15.step_ref
  1.5 0.0 copy-start.3
  1.5 0.0 copy-start.4
  1.5 0.0 copy-start.5
  1.6 0.0 copy-start.6
  1.6 0.0 copy-start.7
  1.6 0.0 copy-start.8
  1.6 0.0 copy-start.9
  1.6 0.0 copy-start.10
  1.6 1.3 %convert_bitcast_fusion.w_out_ref = bf16[192,768]{1,0:T(8,128)(2,1)S(1)} fusion(f32[768,192]{0,1:T(8,128)} %param.25), kind=kLoop, calls=%fused_computation | loop fusion | flops 147456 | bytes 884736 | tf_op jit(solution)/shard_map/transpose | solution.py:736
  2.9 0.0 copy-done
  2.9 0.0 copy-done.2
  2.9 0.0 copy-done.3
  2.9 0.0 copy-done.4
  2.9 0.0 copy-done.5
  3.0 0.0 copy-done.6
  3.0 0.0 copy-done.7
  3.0 0.0 copy-done.8
  3.0 0.0 copy-done.9
  3.0 0.0 copy-start.1
  3.0 1.1 %copy-done.1 = f32[192,768]{1,0:T(8,128)S(1)} copy-done((f32[192,768]{1,0:T(8,128)S(1)}, f32[192,768]{1,0:T(8,128)}, u32[]{:S(2)}) %copy-start.1) | copy-done | bytes 589848
  4.1 100.2 %mixer.1 = bf16[256,384]{1,0:T(8,128)(2,1)S(1)} custom-call(s32[8]{0:T(128)S(1)} %copy-done.6, s32[8]{0:T(128)S(1)} %copy-done.7, bf16[256,384]{1,0:T(8,128)(2,1)S(1)} %copy-done.2, f32[192,768]{1,0:T(8,128)S(1)} %copy-done, f32[192,768]{1,0:T(8,128)S(1)} %copy-done.1, f32[192,256]{1,0:T(8,128)S(1)} %copy-done.3, f32[192,12]{1,0:T(8,128)S(1)} %copy.15.step_ref, ...), custom_call_target="tpu_custom_call" | custom-call | tf_op jit(solution)/shard_map/mixer/pallas_call | solution.py:688
  104.3 0.7 copy.17
  (5 shorter events, 0.0 us)
Async XLA Ops:
  0.0 0.7 copy-start.11
  0.0 2.9 %copy-start = (f32[192,768]{1,0:T(8,128)S(1)}, f32[192,768]{1,0:T(8,128)}, u32[]{:S(2)}) copy-start(f32[192,768]{1,0:T(8,128)} %gate_ref.1) | copy-start | bytes 1769476
  1.5 1.4 %copy-start.2 = (bf16[256,384]{1,0:T(8,128)(2,1)S(1)}, bf16[256,384]{1,0:T(8,128)(2,1)}, u32[]{:S(2)}) copy-start(bf16[256,384]{1,0:T(8,128)(2,1)} %h_ref.1) | copy-start | bytes 589828
  1.5 1.4 %copy-start.3 = (f32[192,256]{1,0:T(8,128)S(1)}, f32[192,256]{1,0:T(8,128)}, u32[]{:S(2)}) copy-start(f32[192,256]{1,0:T(8,128)} %shared_ref.1) | copy-start | bytes 589828
  1.5 1.4 %copy-start.4 = (f32[4,768]{1,0:T(4,128)S(1)}, f32[4,768]{1,0:T(4,128)}, u32[]{:S(2)}) copy-start(f32[4,768]{1,0:T(4,128)} %taps_ref.1) | copy-start | bytes 36868
  1.5 1.4 %copy-start.5 = (f32[4,256]{1,0:T(4,128)S(1)}, f32[4,256]{1,0:T(4,128)}, u32[]{:S(2)}) copy-start(f32[4,256]{1,0:T(4,128)} %shared_taps_ref.1) | copy-start | bytes 12292
  1.6 1.4 %copy-start.6 = (s32[8]{0:T(128)S(1)}, s32[8]{0:T(128)}, u32[]{:S(2)}) copy-start(s32[8]{0:T(128)} %lengths_ref.1) | copy-start | bytes 100
  1.6 1.4 %copy-start.7 = (s32[8]{0:T(128)S(1)}, s32[8]{0:T(128)}, u32[]{:S(2)}) copy-start(s32[8]{0:T(128)} %order_ref.1) | copy-start | bytes 100
  1.6 1.4 %copy-start.8 = (f32[12]{0:T(128)S(1)}, f32[12]{0:T(128)}, u32[]{:S(2)}) copy-start(f32[12]{0:T(128)} %param.21) | copy-start | bytes 148
  1.6 1.4 %copy-start.9 = (f32[12]{0:T(128)S(1)}, f32[12]{0:T(128)}, u32[]{:S(2)}) copy-start(f32[12]{0:T(128)} %param.22) | copy-start | bytes 148
  1.6 1.4 %copy-start.10 = (f32[12]{0:T(128)S(1)}, f32[12]{0:T(128)}, u32[]{:S(2)}) copy-start(f32[12]{0:T(128)} %param.23) | copy-start | bytes 148
  3.0 1.1 %copy-start.1 = (f32[192,768]{1,0:T(8,128)S(1)}, f32[192,768]{1,0:T(8,128)}, u32[]{:S(2)}) copy-start(f32[192,768]{1,0:T(8,128)} %value_ref.1) | copy-start | bytes 1769476

commit v3 on v2

--- a/solution.py
+++ b/solution.py
@@ -323,12 +323,12 @@
 
                     self.going_across(slot, k).start()
 
-    def arrive(self):
+    def arrive(self, planes):
         c = self.at[5]
 
         @pl.loop(0, self.chunks)
         def _(k):
-            for at in range(self.planes):
+            for at in planes:
                 self.going_across(2 * at + 1 - c, k).wait_recv()
 
     def leave(self):
@@ -357,7 +357,7 @@
     planes, heads, inner_total,
     lengths_ref, order_ref, h_ref, gate_ref, value_ref, shared_ref, step_ref, taps_ref,
     shared_taps_ref, bias_ref, log_ref, skip_ref, gain_ref, w_out_ref, out_ref,
-    w_own, w_all, o_all, h_own, h_all, p_own, par, gates, rows_ext, edge_own, edge_got, mixed,
+    w_own, w_all, o_own, o_all, acc, h_own, h_all, p_own, par, gates, rows_ext, edge_own, edge_got, mixed,
     fresh, state_got, state_own, leaving, arrived, sq_leaving, sq_arrived,
     w_got, w_swapped, w_up, w_down, w_across, o_got, o_swapped, o_up, o_down, o_across,
     h_send, h_got, p_sems, edge_sems, state_sems, send, recv, sq_send, sq_recv,
@@ -390,7 +390,7 @@
     greet(planes)
 
     into = Relay(planes, 48, w_own, w_all, (w_got, w_swapped, w_up, w_down, w_across))
-    out_of = Relay(planes, 96, w_out_ref, o_all, (o_got, o_swapped, o_up, o_down, o_across))
+    out_of = Relay(planes, 96, o_own, o_all, (o_got, o_swapped, o_up, o_down, o_across))
     par_local = pltpu.make_async_copy(p_own, par, p_sems.at[0])
     par_swap = remote(p_own, par, p_sems.at[1], p_sems.at[0], seq + 1 - 2 * x, tp + 1 - 2 * c)
     into.start()
@@ -422,10 +422,27 @@
         par_swap.start()
 
     into.turn(0)
+    square = (w_out_ref.shape[0], w_out_ref.shape[0])
+    unit = lax.broadcasted_iota(jnp.int32, square, 0) == lax.broadcasted_iota(jnp.int32, square, 1)
+    o_own[...] = lax.dot_general(
+        w_out_ref[...].astype(bf16), unit.astype(f32).astype(bf16), (((0,), (0,)), ((), ())),
+        preferred_element_type=f32,
+    ).astype(bf16)
     out_of.start()
-    for far in range(1, planes):
+    inside = (z > 0) & (z < planes - 1)
+    outside = jnp.logical_not(inside)
+
+    @pl.when(outside)
+    def _():
+        out_of.turn(0)
+
+    for far in range(1, planes - 1):
         into.turn(far)
-    out_of.turn(0)
+
+    @pl.when(inside)
+    def _():
+        out_of.turn(0)
+        out_of.turn(1)
 
     for quarter in range(4):
         remote(
@@ -441,19 +458,29 @@
     def _():
         par_swap.wait()
 
-    into.arrive()
-
-    def project(start, size):
+    nearest = [jnp.where(z < planes // 2, i, planes - 1 - i) for i in range(planes)]
+
+    def project(start, size, part):
         total = jnp.zeros((tokens, size), f32)
-        for block in range(2 * planes):
-            total = total + jnp.dot(
-                h_all[order_ref[block]], w_all[block, :, start : start + size],
-                preferred_element_type=f32,
-            )
-        return total.astype(bf16)
+        for plane in part:
+            for block in (2 * plane, 2 * plane + 1):
+                total = total + jnp.dot(
+                    h_all[order_ref[block]], w_all[block, :, start : start + size],
+                    preferred_element_type=f32,
+                )
+        return total
+
+    into.arrive(nearest[:-1])
+    for part in range(0, acc.shape[1], 384):
+        acc[:, part : part + 384] = project(part, 384, nearest[:-1])
+    into.turn(planes - 1)
+    into.arrive(nearest[-1:])
+
+    def projected(start, size):
+        return (acc[:, start : start + size] + project(start, size, nearest[-1:])).astype(bf16)
 
     for part in range(0, mix_width, 512):
-        done = project(part, 512)
+        done = projected(part, 512)
         rows_ext[8:, part : part + 512] = done.astype(f32)
         edge_own[:, part : part + 512] = done[tokens - 16 :]
 
@@ -464,8 +491,8 @@
     def _():
         edge(after).start()
 
-    gates[...] = project(mix_width, width)
-    raw = project(step_at, w_own.shape[1] - step_at).astype(f32)
+    gates[...] = projected(mix_width, width)
+    raw = projected(step_at, w_own.shape[1] - step_at).astype(f32)
 
     lane_heads = lax.broadcasted_iota(jnp.int32, (1, 128), 1) < heads
     bias = jnp.where(lane_heads, par[5:6, 0:128], 0.0)
@@ -538,16 +565,30 @@
         weighted, b_rows, (((0,), (0,)), ((), ())), preferred_element_type=f32
     )
 
-    def state(to):
-        return remote(state_own, state_got, state_sems.at[0], state_sems.at[1], *to)
+    parts = 4
+    depth = width // parts
+
+    def state(part, to):
+        at = pl.ds(part * depth, depth)
+        return remote(
+            state_own.at[at], state_got.at[at], state_sems.at[0, part], state_sems.at[1, part], *to
+        )
 
     @pl.when(first)
     def _():
         state_got[...] = jnp.zeros_like(state_got)
         state_own[...] = fresh[...].astype(bf16)
-        state(after).start()
-
-    out_of.turn(1)
+        for part in range(parts):
+            state(part, after).start()
+
+    @pl.when(inside)
+    def _():
+        out_of.turn(2)
+
+    @pl.when(outside)
+    def _():
+        out_of.turn(1)
+
     scores = lax.dot_general(c_rows, b_rows, (((1,), (1,)), ((), ())), preferred_element_type=f32)
     scores = jnp.where(causal, scores, 0.0)
     for head in range(heads):
@@ -560,15 +601,22 @@
 
     @pl.when(jnp.logical_not(first))
     def _():
-        state(before).wait_recv()
-
-        @pl.when(jnp.logical_not(last))
-        def _():
-            state_own[...] = (keep_rows * state_got[...].astype(f32) + fresh[...]).astype(bf16)
-            state(after).start()
-
-    for far in range(2, planes):
-        out_of.turn(far)
+        for part in range(parts):
+            state(part, before).wait_recv()
+
+            @pl.when(jnp.logical_not(last))
+            def _():
+                at = slice(part * depth, (part + 1) * depth)
+                state_own[at] = (
+                    keep_rows[at] * state_got[at].astype(f32) + fresh[at]
+                ).astype(bf16)
+                state(part, after).start()
+
+    @pl.when(outside)
+    def _():
+        for far in range(2, planes):
+            out_of.turn(far)
+
     inter = lax.dot_general(
         c_rows, state_got[...], (((1,), (1,)), ((), ())), preferred_element_type=f32
     ) * over_channels(carry_in)
@@ -584,8 +632,8 @@
     )
     sq_leaving[...] = sums
     scaled = (gated * par[4:5]).astype(bf16)
-    out_of.arrive()
-    columns = 2 * w_out_ref.shape[0]
+    out_of.arrive(range(planes))
+    columns = 2 * w_out_ref.shape[1]
 
     def outward(to):
         return remote(leaving.at[to], arrived.at[share], send.at[to], recv.at[share], 2 * z + c, to)
@@ -625,7 +673,8 @@
     @pl.when(jnp.logical_not(last))
     def _():
         edge(after).wait_send()
-        state(after).wait_send()
+        for part in range(parts):
+            state(part, after).wait_send()
 
     total, sq_total = 0.0, 0.0
     for slot in range(4):
@@ -693,7 +742,9 @@
         scratch_shapes=[
             pltpu.VMEM((rows, in_width), bf16),
             pltpu.VMEM((blocks, rows, in_width), bf16),
+            pltpu.VMEM((out_columns, width), bf16),
             pltpu.VMEM((blocks, out_columns, width), bf16),
+            pltpu.VMEM((tokens, in_width), f32),
             pltpu.VMEM((2, tokens, features // 2), bf16),
             pltpu.VMEM((8, tokens, features // 2), bf16),
             pltpu.VMEM((8, width), f32),
@@ -713,7 +764,7 @@
         ]
         + relay_sems(rows // 48)
         + relay_sems(out_columns // 96)
-        + [dma((4,)), dma((4,)), dma((2,)), dma((2,)), dma((2,))]
+        + [dma((4,)), dma((4,)), dma((2,)), dma((2,)), dma((2, 4))]
         + [dma((4,))] * 4,
         compiler_params=pltpu.CompilerParams(
             collective_id=0, has_side_effects=True, vmem_limit_bytes=50 << 20
@@ -733,7 +784,7 @@
         a_log[None],
         skip_gain[None],
         norm_gain[None],
-        w_out.astype(bf16).T,
+        w_out,
     )
 
 

time: 106 us -> 97.5 us (0.920)
  Pallas kernels: 100 us -> 92.4 us
  local copies, waits for them, and re-layouts: 3.31 us -> 4.65 us
  other arithmetic: 1.29 us -> 0 us
    pallas_call x1, Pallas kernels: 100 us -> 92.4 us  [on_device_paired(): pl.pallas_call(functools.partial(mixer_kernel, planes, heads, width * lax...]
    unnamed x26 -> x27, local copies, waits for them, and re-layouts: 3.3 us -> 4.64 us
    transpose x1 -> x0, other arithmetic: 1.29 us -> none  [on_device_paired(): w_out.astype(bf16)]
where the time goes in v3:
time: 97.5 us; the launch traced here: 97.2 us
  Pallas kernels  92.4 us (95%)
  local copies, waits for them, and re-layouts  4.65 us (5%)
    pallas_call x1, Pallas kernels, on_device_paired(): pl.pallas_call(functools.partial(mixer_kernel, planes, heads, width * lax...  92.4 us
    unnamed x27, local copies, waits for them, and re-layouts  4.64 us

profile of v3, /device:TPU:29, one launch (start us, length us, event | category | flops | bytes accessed | tf_op | source)
XLA Modules:
  0.0 97.2 jit_solution(2356840025131465589)
XLA Ops:
  0.0 0.0 copy-start.11
  0.0 0.7 copy-done.11
  0.7 0.0 copy-start.7
  0.7 0.0 copy-start.8
  0.7 0.0 copy-start.9
  0.7 0.0 copy-start.10
  0.8 0.9 copy.15.step_ref
  1.6 0.0 copy-start.1
  1.6 0.0 copy-start.2
  1.7 1.4 %copy.16.w_out_ref = f32[768,192]{1,0:T(8,128)S(1)} copy(f32[768,192]{0,1:T(8,128)} %param.25) | data formatting | bytes 1179648 | tf_op args[11]
  3.1 0.0 copy-done.4
  3.1 0.0 copy-done.5
  3.1 0.0 copy-done.6
  3.1 0.0 copy-done.7
  3.1 0.0 copy-done.8
  3.1 0.0 copy-done.9
  3.2 0.0 copy-done.10
  3.2 0.0 copy-done
  3.2 0.0 copy-done.1
  3.2 0.0 copy-done.2
  3.2 0.0 copy-start.3
  3.2 0.9 copy-done.3
  4.1 92.4 %mixer.1 = bf16[256,384]{1,0:T(8,128)(2,1)S(1)} custom-call(s32[8]{0:T(128)S(1)} %copy-done.6, s32[8]{0:T(128)S(1)} %copy-done.7, bf16[256,384]{1,0:T(8,128)(2,1)S(1)} %copy-done.2, f32[192,768]{1,0:T(8,128)S(1)} %copy-done, f32[192,768]{1,0:T(8,128)S(1)} %copy-done.1, f32[192,256]{1,0:T(8,128)S(1)} %copy-done.3, f32[192,12]{1,0:T(8,128)S(1)} %copy.15.step_ref, ...), custom_call_target="tpu_custom_call" | custom-call | tf_op jit(solution)/shard_map/mixer/pallas_call | solution.py:737
  96.5 0.7 copy.18
  (5 shorter events, 0.0 us)
Async XLA Ops:
  0.0 0.7 copy-start.11
  0.7 2.4 %copy-start.4 = (f32[4,768]{1,0:T(4,128)S(1)}, f32[4,768]{1,0:T(4,128)}, u32[]{:S(2)}) copy-start(f32[4,768]{1,0:T(4,128)} %taps_ref.1) | copy-start | bytes 36868
  0.7 2.4 %copy-start.5 = (f32[4,256]{1,0:T(4,128)S(1)}, f32[4,256]{1,0:T(4,128)}, u32[]{:S(2)}) copy-start(f32[4,256]{1,0:T(4,128)} %shared_taps_ref.1) | copy-start | bytes 12292
  0.7 2.4 %copy-start.6 = (s32[8]{0:T(128)S(1)}, s32[8]{0:T(128)}, u32[]{:S(2)}) copy-start(s32[8]{0:T(128)} %lengths_ref.1) | copy-start | bytes 100
  0.7 2.4 %copy-start.7 = (s32[8]{0:T(128)S(1)}, s32[8]{0:T(128)}, u32[]{:S(2)}) copy-start(s32[8]{0:T(128)} %order_ref.1) | copy-start | bytes 100
  0.7 2.4 %copy-start.8 = (f32[12]{0:T(128)S(1)}, f32[12]{0:T(128)}, u32[]{:S(2)}) copy-start(f32[12]{0:T(128)} %param.21) | copy-start | bytes 148
  0.7 2.4 %copy-start.9 = (f32[12]{0:T(128)S(1)}, f32[12]{0:T(128)}, u32[]{:S(2)}) copy-start(f32[12]{0:T(128)} %param.22) | copy-start | bytes 148
  0.7 2.4 %copy-start.10 = (f32[12]{0:T(128)S(1)}, f32[12]{0:T(128)}, u32[]{:S(2)}) copy-start(f32[12]{0:T(128)} %param.23) | copy-start | bytes 148
  1.6 1.5 %copy-start = (f32[192,768]{1,0:T(8,128)S(1)}, f32[192,768]{1,0:T(8,128)}, u32[]{:S(2)}) copy-start(f32[192,768]{1,0:T(8,128)} %gate_ref.1) | copy-start | bytes 1769476
  1.6 1.5 %copy-start.1 = (f32[192,768]{1,0:T(8,128)S(1)}, f32[192,768]{1,0:T(8,128)}, u32[]{:S(2)}) copy-start(f32[192,768]{1,0:T(8,128)} %value_ref.1) | copy-start | bytes 1769476
  1.6 1.5 %copy-start.2 = (bf16[256,384]{1,0:T(8,128)(2,1)S(1)}, bf16[256,384]{1,0:T(8,128)(2,1)}, u32[]{:S(2)}) copy-start(bf16[256,384]{1,0:T(8,128)(2,1)} %h_ref.1) | copy-start | bytes 589828
  3.2 0.9 copy-start.3

commit v4 on v3

--- a/solution.py
+++ b/solution.py
@@ -357,10 +357,10 @@
     planes, heads, inner_total,
     lengths_ref, order_ref, h_ref, gate_ref, value_ref, shared_ref, step_ref, taps_ref,
     shared_taps_ref, bias_ref, log_ref, skip_ref, gain_ref, w_out_ref, out_ref,
-    w_own, w_all, o_own, o_all, acc, h_own, h_all, p_own, par, gates, rows_ext, edge_own, edge_got, mixed,
+    w_own, w_all, o_own, o_all, acc, h_own, h_all, p_own, par, gates, rows_ext, edge_own, edge_got, mixed, part_own, part_got,
     fresh, state_got, state_own, leaving, arrived, sq_leaving, sq_arrived,
     w_got, w_swapped, w_up, w_down, w_across, o_got, o_swapped, o_up, o_down, o_across,
-    h_send, h_got, p_sems, edge_sems, state_sems, send, recv, sq_send, sq_recv,
+    h_send, h_got, p_sems, edge_sems, state_sems, part_sems, send, recv, sq_send, sq_recv,
 ):
     f32, bf16 = jnp.float32, jnp.bfloat16
     seq, tp, z, x, y, c = place()
@@ -370,15 +370,26 @@
     after = (seq + 2 * c, tp + 1 - 2 * c)
     tokens, width = h_ref.shape[0], value_ref.shape[1]
     shared_width = shared_ref.shape[1]
-    mix_width, state_size, head_dim = width + shared_width, shared_width // 2, width // heads
+    quarter = shared_width // 4
+    mix_width, state_size, head_dim = width + 2 * quarter, shared_width // 2, width // heads
     half_features = h_ref.shape[1] // 2
-    step_at = mix_width + width
+
+    def quarter_of(array, which):
+        total = jnp.zeros((array.shape[0], quarter), f32)
+        for i in range(4):
+            total = jnp.where(which == i, array[:, i * quarter : (i + 1) * quarter], total)
+        return total
 
     w_own[:, 0:width] = value_ref[...].astype(bf16)
-    w_own[:, width:mix_width] = shared_ref[...].astype(bf16)
-    w_own[:, mix_width:step_at] = gate_ref[...].astype(bf16)
-    w_own[:, step_at:] = jnp.zeros((w_own.shape[0], w_own.shape[1] - step_at), bf16)
-    w_own[:, step_at : step_at + heads] = step_ref[...].astype(bf16)
+    lanes = lax.broadcasted_iota(jnp.int32, (heads, quarter), 1)
+    pick = (lanes == lax.broadcasted_iota(jnp.int32, (heads, quarter), 0)).astype(f32).astype(bf16)
+    steps = lax.dot_general(
+        step_ref[...].astype(bf16), pick, (((0,), (0,)), ((), ())), preferred_element_type=f32
+    )
+    w_own[:, width:mix_width] = jnp.concatenate(
+        [steps, quarter_of(shared_ref[...], tp)], axis=1
+    ).astype(bf16)
+    w_own[:, mix_width:] = gate_ref[...].astype(bf16)
     h_own[0] = h_ref[:, 0:half_features]
     h_own[1] = h_ref[:, half_features:]
     p_own[...] = jnp.zeros_like(p_own)
@@ -422,12 +433,7 @@
         par_swap.start()
 
     into.turn(0)
-    square = (w_out_ref.shape[0], w_out_ref.shape[0])
-    unit = lax.broadcasted_iota(jnp.int32, square, 0) == lax.broadcasted_iota(jnp.int32, square, 1)
-    o_own[...] = lax.dot_general(
-        w_out_ref[...].astype(bf16), unit.astype(f32).astype(bf16), (((0,), (0,)), ((), ())),
-        preferred_element_type=f32,
-    ).astype(bf16)
+    o_own[...] = w_out_ref[...].astype(bf16)
     out_of.start()
     inside = (z > 0) & (z < planes - 1)
     outside = jnp.logical_not(inside)
@@ -444,9 +450,9 @@
         out_of.turn(0)
         out_of.turn(1)
 
-    for quarter in range(4):
+    for held in range(4):
         remote(
-            h_own, h_all.at[pl.ds(2 * quarter, 2)], h_send.at[0], h_got.at[quarter],
+            h_own, h_all.at[pl.ds(2 * held, 2)], h_send.at[0], h_got.at[held],
             seq, tp + 1 - 2 * c,
         ).wait_recv()
 
@@ -472,17 +478,19 @@
 
     into.arrive(nearest[:-1])
     for part in range(0, acc.shape[1], 384):
-        acc[:, part : part + 384] = project(part, 384, nearest[:-1])
+        size = min(384, acc.shape[1] - part)
+        acc[:, part : part + size] = project(part, size, nearest[:-1])
     into.turn(planes - 1)
     into.arrive(nearest[-1:])
 
     def projected(start, size):
         return (acc[:, start : start + size] + project(start, size, nearest[-1:])).astype(bf16)
 
-    for part in range(0, mix_width, 512):
-        done = projected(part, 512)
-        rows_ext[8:, part : part + 512] = done.astype(f32)
-        edge_own[:, part : part + 512] = done[tokens - 16 :]
+    for part in range(0, mix_width, 384):
+        size = min(384, mix_width - part)
+        done = projected(part, size)
+        rows_ext[8:, part : part + size] = done.astype(f32)
+        edge_own[:, part : part + size] = done[tokens - 16 :]
 
     def edge(to):
         return remote(edge_own, edge_got, edge_sems.at[0], edge_sems.at[1], *to)
@@ -492,7 +500,7 @@
         edge(after).start()
 
     gates[...] = projected(mix_width, width)
-    raw = projected(step_at, w_own.shape[1] - step_at).astype(f32)
+    raw = rows_ext[8:, width:mix_width]
 
     lane_heads = lax.broadcasted_iota(jnp.int32, (1, 128), 1) < heads
     bias = jnp.where(lane_heads, par[5:6, 0:128], 0.0)
@@ -555,8 +563,30 @@
             total = total + jnp.where(counted[:, 0:1], term, 0.0)
         return jax.nn.silu(total).astype(bf16)
 
+    shared_taps = quarter_of(shared_taps_ref[...], share)
+    part_own[...] = convolve(
+        width, 2 * quarter, jnp.concatenate([jnp.zeros_like(shared_taps), shared_taps], axis=1)
+    )
+
+    def piece(dx, dy):
+        return remote(
+            part_own, part_got.at[share], part_sems.at[0, 2 * dy + dx], part_sems.at[1, share],
+            2 * z + (x + dx) % 2, 2 * ((y + dy) % 2) + c,
+        )
+
+    pieces = ((1, 1), (1, 0), (0, 1))
+    for dx, dy in pieces:
+        piece(dx, dy).start()
+    part_got[share] = part_own[...]
     mixed[:, 0:width] = convolve(0, width, par[0:4])
-    mixed[:, width:] = convolve(width, shared_width, shared_taps_ref[...])
+    for dx, dy in pieces:
+        source = 2 * ((y + dy) % 2) + (x + dx) % 2
+        remote(
+            part_own, part_got.at[source], part_sems.at[0, 0], part_sems.at[1, source],
+            2 * z + (x + dx) % 2, 2 * ((y + dy) % 2) + c,
+        ).wait_recv()
+    for i in range(4):
+        mixed[:, width + i * quarter : width + (i + 1) * quarter] = part_got[i][:, quarter:]
     values = mixed[:, 0:width]
     b_rows = mixed[:, width : width + state_size]
     c_rows = mixed[:, width + state_size :]
@@ -614,7 +644,7 @@
 
     @pl.when(outside)
     def _():
-        for far in range(2, planes):
+        for far in range(2, planes - 1):
             out_of.turn(far)
 
     inter = lax.dot_general(
@@ -632,8 +662,7 @@
     )
     sq_leaving[...] = sums
     scaled = (gated * par[4:5]).astype(bf16)
-    out_of.arrive(range(planes))
-    columns = 2 * w_out_ref.shape[1]
+    columns = 2 * w_out_ref.shape[0]
 
     def outward(to):
         return remote(leaving.at[to], arrived.at[share], send.at[to], recv.at[share], 2 * z + c, to)
@@ -643,9 +672,15 @@
             sq_leaving, sq_arrived.at[share], sq_send.at[to], sq_recv.at[share], 2 * z + c, to
         )
 
-    for to in range(4):
+    for to in nearest:
+        if to is nearest[-1]:
+            @pl.when(outside)
+            def _():
+                out_of.turn(planes - 1)
+
+        out_of.arrive([to])
         product = lax.dot_general(
-            scaled, o_all[2 * to : 2 * to + 2].reshape(columns, width),
+            scaled, o_all[pl.ds(2 * to, 2)].reshape(columns, width),
             (((1,), (1,)), ((), ())), preferred_element_type=f32,
         ).astype(bf16)
         itself = (x == c) & (tp == to)
@@ -656,12 +691,14 @@
             sq_arrived[share] = sums
 
         @pl.when(jnp.logical_not(itself))
-        def _():
+        def _(to=to, product=product):
             leaving[to] = product
             outward(to).start()
             squares(to).start()
 
     into.leave()
+    for dx, dy in pieces:
+        piece(dx, dy).wait_send()
     out_of.leave()
     for to in range(4):
         itself = (x == c) & (x == to // 2) & (y == to % 2)
@@ -724,8 +761,8 @@
     tokens, features = hidden_in.shape
     rows, width = w_in_value.shape
     shared_width, heads = w_in_shared.shape[1], dt_bias.shape[0]
-    mix_width = width + shared_width
-    in_width = mix_width + width + 128
+    mix_width = width + shared_width // 2
+    in_width = mix_width + width
     state_size = shared_width // 2
     out_columns = w_out.shape[1]
     f32, bf16, dma = jnp.float32, jnp.bfloat16, pltpu.SemaphoreType.DMA
@@ -753,7 +790,9 @@
             pltpu.VMEM((tokens + 8, mix_width), f32),
             pltpu.VMEM((16, mix_width), bf16),
             pltpu.VMEM((16, mix_width), bf16),
-            pltpu.VMEM((tokens, mix_width), bf16),
+            pltpu.VMEM((tokens, width + shared_width), bf16),
+            pltpu.VMEM((tokens, shared_width // 2), bf16),
+            pltpu.VMEM((4, tokens, shared_width // 2), bf16),
             pltpu.VMEM((width, state_size), f32),
             pltpu.VMEM((width, state_size), bf16),
             pltpu.VMEM((width, state_size), bf16),
@@ -764,7 +803,7 @@
         ]
         + relay_sems(rows // 48)
         + relay_sems(out_columns // 96)
-        + [dma((4,)), dma((4,)), dma((2,)), dma((2,)), dma((2, 4))]
+        + [dma((4,)), dma((4,)), dma((2,)), dma((2,)), dma((2, 4)), dma((2, 4))]
         + [dma((4,))] * 4,
         compiler_params=pltpu.CompilerParams(
             collective_id=0, has_side_effects=True, vmem_limit_bytes=50 << 20
@@ -777,14 +816,14 @@
         w_in_gate,
         w_in_value,
         w_in_shared,
-        w_in_step,
+        w_in_step.T,
         conv_value,
         conv_shared,
         dt_bias[None],
         a_log[None],
         skip_gain[None],
         norm_gain[None],
-        w_out,
+        w_out.T,
     )
 
 

time: 97.5 us -> 102 us (1.046)
  the two profiles are of different devices: /device:TPU:29 before, /device:TPU:26 now
where the time goes in v4:
time: 102 us
  Pallas kernels  90.7 us (89%)
  local copies, waits for them, and re-layouts  11.1 us (11%)
    pallas_call x1, Pallas kernels, on_device_paired(): pl.pallas_call(functools.partial(mixer_kernel, planes, heads, width * lax...  90.7 us
    unnamed x27, local copies, waits for them, and re-layouts  10.4 us

profile of v4, /device:TPU:26, one launch (start us, length us, event | category | flops | bytes accessed | tf_op | source)
XLA Modules:
  0.0 101.8 jit_solution(13289098260545997412)
XLA Ops:
  0.0 0.0 copy-start.5
  0.0 0.7 broadcast_in_dim.15.gain_ref
  0.7 0.0 copy-done.5
  0.7 0.0 copy-start
  0.7 1.1 %copy-done = f32[192,768]{1,0:T(8,128)S(1)} copy-done((f32[192,768]{1,0:T(8,128)S(1)}, f32[192,768]{1,0:T(8,128)}, u32[]{:S(2)}) %copy-start) | copy-done | bytes 589848
  1.8 0.0 copy-start.1
  1.8 1.1 %copy-done.1 = f32[192,768]{1,0:T(8,128)S(1)} copy-done((f32[192,768]{1,0:T(8,128)S(1)}, f32[192,768]{1,0:T(8,128)}, u32[]{:S(2)}) %copy-start.1) | copy-done | bytes 589848
  2.8 0.0 copy-start.2
  2.9 1.1 %copy-done.2 = f32[768,192]{0,1:T(8,128)S(1)} copy-done((f32[768,192]{0,1:T(8,128)S(1)}, f32[768,192]{0,1:T(8,128)}, u32[]{:S(2)}) %copy-start.2) | copy-done | bytes 589848
  3.9 0.0 copy-start.3
  3.9 0.9 copy-done.3
  4.8 0.0 copy-start.4
  4.8 0.9 copy-done.4
  5.8 0.0 copy-start.6
  5.8 0.7 copy-done.6
  6.5 0.0 copy-start.7
  6.5 0.7 copy-done.7
  7.2 0.7 copy-done.8
  7.8 0.7 copy-done.9
  8.5 0.7 copy-done.10
  9.1 0.7 copy-done.11
  9.8 0.7 copy-done.12
  10.4 90.7 %mixer.1 = bf16[256,384]{1,0:T(8,128)(2,1)S(1)} custom-call(s32[8]{0:T(128)S(1)} %copy-done.8, s32[8]{0:T(128)S(1)} %copy-done.9, bf16[256,384]{1,0:T(8,128)(2,1)S(1)} %copy-done.3, f32[192,768]{1,0:T(8,128)S(1)} %copy-done, f32[192,768]{1,0:T(8,128)S(1)} %copy-done.1, f32[192,256]{1,0:T(8,128)S(1)} %copy-done.4, f32[12,192]{1,0:T(8,128)S(1)} %bitcast.6, ...), custom_call_target="tpu_custom_call" | custom-call | tf_op jit(solution)/shard_map/mixer/pallas_call | solution.py:774
  101.1 0.7 copy.16
  (5 shorter events, 0.0 us)
Async XLA Ops:
  0.0 0.7 copy-start.5
  0.7 1.1 %copy-start = (f32[192,768]{1,0:T(8,128)S(1)}, f32[192,768]{1,0:T(8,128)}, u32[]{:S(2)}) copy-start(f32[192,768]{1,0:T(8,128)} %gate_ref.1) | copy-start | bytes 1769476
  1.8 1.1 %copy-start.1 = (f32[192,768]{1,0:T(8,128)S(1)}, f32[192,768]{1,0:T(8,128)}, u32[]{:S(2)}) copy-start(f32[192,768]{1,0:T(8,128)} %value_ref.1) | copy-start | bytes 1769476
  2.8 1.1 %copy-start.2 = (f32[768,192]{0,1:T(8,128)S(1)}, f32[768,192]{0,1:T(8,128)}, u32[]{:S(2)}) copy-start(f32[768,192]{0,1:T(8,128)} %param.25) | copy-start | bytes 1769476
  3.9 0.9 copy-start.3
  4.8 0.9 copy-start.4
  5.8 0.7 copy-start.6
  6.5 0.7 copy-start.7
  7.2 0.7 copy-start.8
  7.8 0.7 copy-start.9
  8.5 0.7 copy-start.10
  9.1 0.7 copy-start.11
  9.8 0.7 copy-start.12

commit v5 on v4

--- a/solution.py
+++ b/solution.py
@@ -355,13 +355,29 @@
 
 def mixer_kernel(
     planes, heads, inner_total,
-    lengths_ref, order_ref, h_ref, gate_ref, value_ref, shared_ref, step_ref, taps_ref,
-    shared_taps_ref, bias_ref, log_ref, skip_ref, gain_ref, w_out_ref, out_ref,
-    w_own, w_all, o_own, o_all, acc, h_own, h_all, p_own, par, gates, rows_ext, edge_own, edge_got, mixed, part_own, part_got,
+    lengths_ref, order_ref, *refs,
+):
+    arguments, (out_ref, *held) = refs[:12], refs[12:]
+    inside_refs, (load_sems, *scratch) = held[:12], held[12:]
+    (
+        h_ref, gate_ref, value_ref, shared_ref, step_ref, taps_ref,
+        shared_taps_ref, bias_ref, log_ref, skip_ref, gain_ref, w_out_ref,
+    ) = inside_refs
+    (
+        w_own, w_all, o_own, o_all, acc, h_own, h_all, p_own, par, gates, rows_ext, edge_own, edge_got, mixed, part_own, part_got,
     fresh, state_got, state_own, leaving, arrived, sq_leaving, sq_arrived,
     w_got, w_swapped, w_up, w_down, w_across, o_got, o_swapped, o_up, o_down, o_across,
     h_send, h_got, p_sems, edge_sems, state_sems, part_sems, send, recv, sq_send, sq_recv,
-):
+    ) = scratch
+    loads = [
+        pltpu.make_async_copy(argument, inside, load_sems.at[i])
+        for i, (argument, inside) in enumerate(zip(arguments, inside_refs))
+    ]
+    for load in loads:
+        load.start()
+    greet(planes)
+    for load in loads:
+        load.wait()
     f32, bf16 = jnp.float32, jnp.bfloat16
     seq, tp, z, x, y, c = place()
     share = 2 * y + x
@@ -398,7 +414,6 @@
     p_own[5:6, 0:heads] = bias_ref[...]
     p_own[6:7, 0:heads] = log_ref[...]
     p_own[7:8, 0:heads] = skip_ref[...]
-    greet(planes)
 
     into = Relay(planes, 48, w_own, w_all, (w_got, w_swapped, w_up, w_down, w_across))
     out_of = Relay(planes, 96, o_own, o_all, (o_got, o_swapped, o_up, o_down, o_across))
@@ -771,12 +786,28 @@
     def relay_sems(chunks):
         return [dma((blocks, chunks)), dma((chunks,))] + [dma((planes, chunks))] * 3
 
+    arguments = (
+        hidden_in,
+        w_in_gate,
+        w_in_value,
+        w_in_shared,
+        w_in_step.T,
+        conv_value,
+        conv_shared,
+        dt_bias[None],
+        a_log[None],
+        skip_gain[None],
+        norm_gain[None],
+        w_out.T,
+    )
     return pl.pallas_call(
         functools.partial(mixer_kernel, planes, heads, width * lax.axis_size("tp")),
         out_shape=jax.ShapeDtypeStruct((tokens, features), bf16),
-        in_specs=[smem] * 2 + [vmem] * 12,
+        in_specs=[smem] * 2 + [pl.BlockSpec(memory_space=pl.ANY)] * len(arguments),
         out_specs=vmem,
-        scratch_shapes=[
+        scratch_shapes=[pltpu.VMEM(array.shape, array.dtype) for array in arguments]
+        + [
+            dma((len(arguments),)),
             pltpu.VMEM((rows, in_width), bf16),
             pltpu.VMEM((blocks, rows, in_width), bf16),
             pltpu.VMEM((out_columns, width), bf16),
@@ -806,25 +837,10 @@
         + [dma((4,)), dma((4,)), dma((2,)), dma((2,)), dma((2, 4)), dma((2, 4))]
         + [dma((4,))] * 4,
         compiler_params=pltpu.CompilerParams(
-            collective_id=0, has_side_effects=True, vmem_limit_bytes=50 << 20
+            collective_id=0, has_side_effects=True, vmem_limit_bytes=58 << 20
         ),
         name="mixer",
-    )(
-        prompt_lengths,
-        row_blocks,
-        hidden_in,
-        w_in_gate,
-        w_in_value,
-        w_in_shared,
-        w_in_step.T,
-        conv_value,
-        conv_shared,
-        dt_bias[None],
-        a_log[None],
-        skip_gain[None],
-        norm_gain[None],
-        w_out.T,
-    )
+    )(prompt_lengths, row_blocks, *arguments)
 
 
 def paired(mesh):

time: 102 us -> 94.8 us (0.929)
  local copies, waits for them, and re-layouts: 11.1 us -> 2.89 us
    unnamed x27 -> x3, local copies, waits for them, and re-layouts: 10.4 us -> 2.31 us
where the time goes in v5:
time: 94.8 us; the launch traced here: 94.6 us
  Pallas kernels  91.7 us (97%)
  local copies, waits for them, and re-layouts  2.89 us (3%)
    pallas_call x1, Pallas kernels, on_device_paired(): pl.pallas_call(functools.partial(mixer_kernel, planes, heads, width * lax...  91.7 us
    unnamed x3, local copies, waits for them, and re-layouts  2.31 us

profile of v5, /device:TPU:26, one launch (start us, length us, event | category | flops | bytes accessed | tf_op | source)
XLA Modules:
  0.0 94.6 jit_solution(6243062210860901195)
XLA Ops:
  0.0 0.0 copy-start
  0.0 0.7 copy-done
  0.7 0.6 broadcast_in_dim.15.refs_10_
  1.3 91.7 %mixer.1 = bf16[256,384]{1,0:T(8,128)(2,1)} custom-call(s32[8]{0:T(128)} %lengths_ref.1, s32[8]{0:T(128)} %order_ref.1, bf16[256,384]{1,0:T(8,128)(2,1)} %refs_0_.1, f32[192,768]{1,0:T(8,128)} %refs_1_.1, f32[192,768]{1,0:T(8,128)} %refs_2_.1, f32[192,256]{1,0:T(8,128)} %refs_3_.1, f32[12,192]{1,0:T(8,128)} %bitcast.6, f32[4,768]{1,0:T(4,128)} %refs_5_.1, ...), custom_call_target="tpu_custom_call" | custom-call | tf_op jit(solution)/shard_map/mixer/pallas_call | solution.py:803
  93.0 1.6 %copy.16 = bf16[256,384]{1,0:T(8,128)(2,1)} copy(bf16[256,384]{1,0:T(8,128)(2,1)} %mixer.1) | data formatting | bytes 393216
Async XLA Ops:
  0.0 0.7 copy-start
